TPU v7x, 32 devices: a whole 2x2x4 slice. The times are simulated.
32 devices in a mesh: seq: 16 (over z, y, core), head: 2 (over x).
Axes of the slice: x: 2, y: 2, z: 4, core: 2. Of those that a mesh axis runs over, the one named last changes fastest.
Arguments:
- queries: bfloat16 [2048, 3072], P(('seq', 'head')), may hold values from -6 to 6
- keys: bfloat16 [2048, 3072], P(('seq', 'head')), may hold values from -6 to 6
- values: bfloat16 [2048, 3072], P(('seq', 'head')), may hold values from -6 to 6
- counts: int32 [4], replicated, may hold values from 256 to 512, as said below
- plan: int32 [4], replicated, may hold values from 0 to 7
- group_mask: int32 [4, 4], replicated, may hold values from 0 to 1, as said below
- gate_table: float32 [8, 3072], replicated, may hold values from -6 to 6
Outputs:
- attended: bfloat16 [2048, 3072], P(('seq', 'head'))
Inputs may be any that keep to these rules, and one draw needn't show every extreme that they name: `counts`: every group's count is at least half of 512; some group is full. `group_mask`: the diagonal is 1 and every entry above it is 0.
All inputs are finite; a program needn't handle non-finite values.
Results may differ from a plain program's by a relative error of at most 0.0046.
Values may be sent and summed in bfloat16 or wider, within the bound.
No kernel may reach another device: no remote copies, remote signals or barrier semaphores. Data moves between devices by JAX's collectives and lax.ppermute only.
A program may use at most 128 MiB of HBM per device.

v0:
```python
import math

import jax
import jax.numpy as jnp
from jax import lax
from jax.sharding import PartitionSpec as P

HEAD_DIM = 128
GROUPS = 4
LEVELS = 8


def lookup(table, index):
    hits = index[:, None] == jnp.arange(table.shape[0], dtype=jnp.int32)[None, :]
    return jnp.sum(jnp.where(hits, table[None, :], 0), axis=1)


def attend(
    work_q, k_local, v_local, row_group, row_pos, counts, plan, group_mask, gate_slice, group_tok
):
    rows = work_q.shape[0]
    width = work_q.shape[1]
    heads_here = width // HEAD_DIM
    scale = 1.0 / math.sqrt(HEAD_DIM)
    q_three = work_q.reshape(rows, heads_here, HEAD_DIM)
    row_onehot = (row_group[:, None] == jnp.arange(GROUPS, dtype=jnp.int32)[None, :]).astype(
        jnp.float32
    )
    mask_rows = jnp.dot(row_onehot, group_mask.astype(jnp.float32))
    k_piece = lax.all_gather(k_local, "seq", axis=0, tiled=True)
    v_piece = lax.all_gather(v_local, "seq", axis=0, tiled=True)
    count = k_piece.shape[0]
    index = jnp.arange(count, dtype=jnp.int32)
    k_group = index // group_tok
    k_pos = index % group_tok
    k_onehot = (k_group[:, None] == jnp.arange(GROUPS, dtype=jnp.int32)[None, :]).astype(
        jnp.float32
    )
    k_valid = k_pos < lookup(counts, k_group)
    allowed = (jnp.dot(mask_rows, k_onehot.T) > 0.5) & k_valid[None, :]
    running = jnp.full((heads_here, rows), -1e30, jnp.float32)
    k_three = k_piece.reshape(count, heads_here, HEAD_DIM)
    v_three = v_piece.reshape(count, heads_here, HEAD_DIM)
    scores = (
        jnp.einsum("qhd,khd->hqk", q_three, k_three, preferred_element_type=jnp.float32) * scale
    )
    scores = jnp.where(allowed[None], scores, jnp.float32(-1e30))
    newest = jnp.maximum(running, jnp.max(scores, axis=2))
    weights = jnp.exp(scores - newest[:, :, None]) * allowed[None].astype(jnp.float32)
    total = jnp.sum(weights, axis=2)
    rounded = weights.astype(jnp.bfloat16)
    accum = jnp.einsum("hqk,khd->hqd", rounded, v_three, preferred_element_type=jnp.float32)
    running, total, accum = (newest, total, accum)
    mixed = accum / total[:, :, None]
    mixed = jnp.transpose(mixed, (1, 0, 2)).reshape(rows, width)
    level_rows = lookup(plan, row_group)
    level_hits = level_rows[:, None] == jnp.arange(LEVELS, dtype=jnp.int32)[None, :]
    gates = jnp.sum(
        jnp.where(level_hits[:, :, None], gate_slice[None, :, :], jnp.float32(0.0)), axis=1
    )
    live = row_pos < lookup(counts, row_group)
    return jnp.where(live[:, None], mixed * gates, jnp.float32(0.0)).astype(jnp.bfloat16)


def on_device(queries, keys, values, counts, plan, group_mask, gate_table):
    n_seq = lax.axis_size("seq")
    n_head = lax.axis_size("head")
    per_group = n_seq // GROUPS
    tok_dev = queries.shape[0] * n_head
    group_tok = tok_dev * per_group
    q_local, k_local, v_local = (
        lax.all_to_all(queries, "head", split_axis=1, concat_axis=0, tiled=True),
        lax.all_to_all(keys, "head", split_axis=1, concat_axis=0, tiled=True),
        lax.all_to_all(values, "head", split_axis=1, concat_axis=0, tiled=True),
    )
    width = q_local.shape[1]
    seq_index = lax.axis_index("seq")
    own_group = seq_index // per_group
    positions = seq_index % per_group * tok_dev + jnp.arange(tok_dev, dtype=jnp.int32)
    gate_slice = lax.dynamic_slice_in_dim(gate_table, lax.axis_index("head") * width, width, 1)
    row_group = jnp.full((tok_dev,), own_group, jnp.int32)
    result = attend(
        q_local,
        k_local,
        v_local,
        row_group,
        positions,
        counts,
        plan,
        group_mask,
        gate_slice,
        group_tok,
    )
    return lax.all_to_all(result, "head", split_axis=0, concat_axis=1, tiled=True)


def solution(mesh):
    in_specs = (
        P(("seq", "head"), None),
        P(("seq", "head"), None),
        P(("seq", "head"), None),
        P(),
        P(),
        P(),
        P(),
    )
    out_specs = P(("seq", "head"), None)
    return jax.shard_map(
        on_device, mesh=mesh, in_specs=in_specs, out_specs=out_specs, check_vma=False
    )
```

profile of v0, /device:TPU:1, one launch (start us, length us, event | category | flops | bytes accessed | tf_op | source)
XLA Modules:
  0.0 179.8 jit_solution(5903753862884938549)
XLA Ops:
  6.5 0.0 copy-start
  6.5 0.0 all-gather.3.cloned.1.call-start
  6.5 1.1 copy.60
  7.6 9.9 %all_to_all.70 = bf16[64,2,1536]{2,0,1:T(8,128)(2,1)} all-to-all(bf16[64,2,1536]{2,0,1:T(8,128)(2,1)S(1)} %bitcast.39), channel_id=1, replica_groups=mesh['seq'=16,'head'=2] {'head'}, dimensions={1} | all-to-all | bytes 786432 | tf_op jit(solution)/shard_map/all_to_all | solution.py:73
  17.5 0.0 all-gather.3.cloned.1.call-update
  17.5 0.0 all-gather.5.cloned.1.call-start
  17.6 1.0 copy.59
  18.6 8.4 %all_to_all.71 = bf16[64,2,1536]{2,0,1:T(8,128)(2,1)} all-to-all(bf16[64,2,1536]{2,0,1:T(8,128)(2,1)S(1)} %bitcast.40), channel_id=1, replica_groups=mesh['seq'=16,'head'=2] {'head'}, dimensions={1} | all-to-all | bytes 786432 | tf_op jit(solution)/shard_map/all_to_all | solution.py:74
  27.0 0.0 all-gather.5.cloned.1.call-update
  27.0 1.8 copy.61
  28.8 3.5 %all-to-all-start = ((bf16[64,2,1536]{2,0,1:T(8,128)(2,1)}), bf16[64,2,1536]{2,0,1:T(8,128)(2,1)S(1)}, u32[]{:S(2)}, u32[]{:S(2)}) async-start(bf16[64,2,1536]{2,0,1:T(8,128)(2,1)} %bitcast.31), calls=%async_computation | async-start | bytes 786432 | tf_op jit(solution)/shard_map/all_to_all | solution.py:72
  32.3 0.8 select_reduce_fusion.3
  33.0 0.1 reduce_sum.50
  33.1 0.7 select_reduce_fusion.1
  33.9 0.1 iota_compare_fusion
  34.0 0.0 copy-done
  34.0 1.8 select_reduce_fusion
  35.8 2.3 %fusion.32 = (f32[128,2048]{1,0:T(8,128)}, pred[128,2048]{1,0:T(8,128)(4,1)S(1)}) fusion(pred[2048]{0:T(1024)(128)(4,1)S(1)} %fusion.24, s32[2048]{0:T(1024)S(1)} %add_select_fusion, s32[4,4]{1,0:T(4,128)} %param.12, pred[4]{0:T(512)(128)(4,1)S(1)} %iota_compare_fusion.3), kind=kOutput, calls=%fused_computation.45 | convolution fusion | flops 2895888 | bytes 1321028 | tf_op jit(solution)/shard_map/dot_general | solution.py:40
  38.1 0.0 all-to-all-done
  38.1 0.3 reshape.96
  38.4 42.7 %all-gather.3.cloned.1.call-done = bf16[2048,1536]{1,0:T(8,128)(2,1)} async-done(((bf16[128,1536]{1,0:T(8,128)(2,1)}), bf16[2048,1536]{1,0:T(8,128)(2,1)}) %all-gather.3.cloned.1.call-update) | async-done | bytes 6291472 | tf_op jit(solution)/shard_map/all_gather | solution.py:30
  81.2 8.7 %copy.38 = bf16[2048,1536]{0,1:T(8,128)(2,1)} copy(bf16[2048,1536]{1,0:T(8,128)(2,1)} %all-gather.3.cloned.1.call-done) | data formatting | bytes 12582912 | tf_op jit(solution)/shard_map/all_gather | solution.py:30
  89.8 0.0 copy-start.2
  89.8 5.4 %fusion = (f32[12,128]{1,0:T(8,128)S(1)}, f32[12,128,2048]{2,1,0:T(8,128)S(1)}) fusion(pred[128,2048]{1,0:T(8,128)(4,1)S(1)} %get-tuple-element.8, bf16[2048,12,128]{0,2,1:T(8,128)(2,1)} %bitcast.32, bf16[128,12,128]{2,1,0:T(8,128)(2,1)S(1)} %reshape.96), kind=kOutput, calls=%fused_computation.2 | convolution fusion | flops 814742016 | bytes 19535872 | tf_op jit(solution)/shard_map/qhd,khd->hqk/dot_general | solution.py:45
  95.3 0.0 copy-start.1
  95.3 4.5 %copy-done.1 = f32[12,128,2048]{2,1,0:T(8,128)} copy-done((f32[12,128,2048]{2,1,0:T(8,128)}, f32[12,128,2048]{2,1,0:T(8,128)S(1)}, u32[]{:S(2)}) %copy-start.1) | copy-done | bytes 12582936
  99.8 0.0 copy-done.2
  99.8 3.8 %fusion.1 = f32[12,128]{1,0:T(8,128)S(1)} fusion(f32[12,128,2048]{2,1,0:T(8,128)S(1)} %get-tuple-element.10, f32[128,2048]{1,0:T(8,128)S(1)} %copy-done.2, f32[12,128]{1,0:T(8,128)S(1)} %broadcast_maximum_fusion, pred[128,2048]{1,0:T(8,128)(4,1)S(1)} %get-tuple-element.8), kind=kLoop, calls=%fused_computation.3 | loop fusion | flops 15727104 | bytes 13905920 | tf_op jit(solution)/shard_map/reduce_sum | solution.py:50
  103.6 40.3 %all-gather.5.cloned.1.call-done = bf16[2048,1536]{1,0:T(8,128)(2,1)} async-done(((bf16[128,1536]{1,0:T(8,128)(2,1)}), bf16[2048,1536]{1,0:T(8,128)(2,1)}) %all-gather.5.cloned.1.call-update) | async-done | bytes 6291472 | tf_op jit(solution)/shard_map/all_gather | solution.py:31
  143.9 8.7 %copy.42 = bf16[2048,1536]{0,1:T(8,128)(2,1)} copy(bf16[2048,1536]{1,0:T(8,128)(2,1)} %all-gather.5.cloned.1.call-done) | data formatting | bytes 12582912 | tf_op jit(solution)/shard_map/all_gather | solution.py:31
  152.6 10.0 %fusion.12 = f32[128,12,128]{2,0,1:T(8,128)S(1)} fusion(bf16[2048,12,128]{0,2,1:T(8,128)(2,1)} %bitcast.33, f32[12,128,2048]{2,1,0:T(8,128)} %copy-done.1, f32[128,2048]{1,0:T(8,128)S(1)} %copy-done.2, f32[12,128]{1,0:T(8,128)S(1)} %broadcast_maximum_fusion, pred[128,2048]{1,0:T(8,128)(4,1)S(1)} %get-tuple-element.8, f32[128,12]{0,1:T(8,128)S(1)} %bitcast.44), kind=kOutput, calls=%fused_computation.12 | convolution fusion | flops 821231616 | bytes 20983808 | tf_op jit(solution)/shard_map/hqk,khd->hqd/dot_general | solution.py:52
  162.7 0.5 copy.44
  163.2 0.1 reshape.99
  163.3 0.2 select_convert_fusion
  163.4 8.7 %all_to_all.72 = bf16[2,64,1536]{2,1,0:T(8,128)(2,1)S(1)} all-to-all(bf16[2,64,1536]{2,1,0:T(8,128)(2,1)S(1)} %select_convert_fusion), channel_id=1, replica_groups=mesh['seq'=16,'head'=2] {'head'}, dimensions={0} | all-to-all | bytes 786432 | tf_op jit(solution)/shard_map/all_to_all | solution.py:94
  172.2 0.8 copy.51
  (6 shorter events, 0.0 us)
Async XLA Ops:
  6.5 27.5 %copy-start = (f32[8,3072]{1,0:T(8,128)S(1)}, f32[8,3072]{1,0:T(8,128)}, u32[]{:S(2)}) copy-start(f32[8,3072]{1,0:T(8,128)} %param.13) | copy-start | bytes 294916
  6.5 74.6 %all-gather.3.cloned.1.call-start = ((), (), s32[]{:S(2)}) async-start(), calls=%async_computation.4 | async-start | bytes 6684672 | tf_op jit(solution)/shard_map/all_gather | solution.py:30
  17.5 126.4 %all-gather.5.cloned.1.call-start = ((), (), s32[]{:S(2)}) async-start(), calls=%async_computation.5 | async-start | bytes 6684672 | tf_op jit(solution)/shard_map/all_gather | solution.py:31
  28.8 9.3 %all-to-all-start = ((bf16[64,2,1536]{2,0,1:T(8,128)(2,1)}), bf16[64,2,1536]{2,0,1:T(8,128)(2,1)S(1)}, u32[]{:S(2)}, u32[]{:S(2)}) async-start(bf16[64,2,1536]{2,0,1:T(8,128)(2,1)} %bitcast.31), calls=%async_computation | async-start | bytes 786432 | tf_op jit(solution)/shard_map/all_to_all | solution.py:72
  89.8 10.0 %copy-start.2 = (f32[128,2048]{1,0:T(8,128)S(1)}, f32[128,2048]{1,0:T(8,128)}, u32[]{:S(2)}) copy-start(f32[128,2048]{1,0:T(8,128)} %get-tuple-element.7) | copy-start | bytes 3145732
  95.3 4.6 %copy-start.1 = (f32[12,128,2048]{2,1,0:T(8,128)}, f32[12,128,2048]{2,1,0:T(8,128)S(1)}, u32[]{:S(2)}) copy-start(f32[12,128,2048]{2,1,0:T(8,128)S(1)} %get-tuple-element.10) | copy-start | bytes 37748740
Sparse Core Ops, SparseCore 0:
  17.6 63.4 all-gather.2
  83.4 60.4 all-gather.4
where the time goes:
time: 182 us; the launch traced here: 180 us
  waiting for transfers between devices  83.1 us (46%)
  local copies, waits for them, and re-layouts  27.5 us (15%)
  blocking collectives  27 us (15%)
  matrix products  17.8 us (10%)
  between operations  13.6 us (7%)
  other arithmetic  7.35 us (4%)
  starting transfers between devices  3.51 us (2%)
    all_gather x1, waiting for transfers between devices, attend(): k_piece = lax.all_gather(k_local, 'seq', axis=0, tiled=True)  42.7 us
    all_gather x1, waiting for transfers between devices, attend(): v_piece = lax.all_gather(v_local, 'seq', axis=0, tiled=True)  40.3 us
    dot_general x1, matrix products, attend(): jnp.einsum('hqk,khd->hqd', rounded, v_three, preferred_element_type=jnp.f...  10 us
    all_to_all x1, blocking collectives, on_device(): lax.all_to_all(keys, 'head', split_axis=1, concat_axis=0, tiled=True)  9.88 us
    all_to_all x1, blocking collectives, on_device(): lax.all_to_all(result, 'head', split_axis=0, concat_axis=1, tiled=True)  8.71 us
    all_gather x1, local copies, waits for them, and re-layouts, attend(): v_piece = lax.all_gather(v_local, 'seq', axis=0, tiled=True)  8.7 us
    all_gather x1, local copies, waits for them, and re-layouts, attend(): k_piece = lax.all_gather(k_local, 'seq', axis=0, tiled=True)  8.66 us
    all_to_all x1, blocking collectives, on_device(): lax.all_to_all(values, 'head', split_axis=1, concat_axis=0, tiled=True)  8.39 us
  transfers between devices with their start and end apart: 3, of which 2 were waited for; matrix products, arithmetic and copies ran while one was open for 15% of the time, Pallas kernels for 0%

commit v1 on v0

--- a/solution.py
+++ b/solution.py
@@ -1,8 +1,11 @@
+import functools
 import math
 
 import jax
 import jax.numpy as jnp
 from jax import lax
+from jax.experimental import pallas as pl
+from jax.experimental.pallas import tpu as pltpu
 from jax.sharding import PartitionSpec as P
 
 HEAD_DIM = 128
@@ -62,7 +65,7 @@
     return jnp.where(live[:, None], mixed * gates, jnp.float32(0.0)).astype(jnp.bfloat16)
 
 
-def on_device(queries, keys, values, counts, plan, group_mask, gate_table):
+def gathered(queries, keys, values, counts, plan, group_mask, gate_table):
     n_seq = lax.axis_size("seq")
     n_head = lax.axis_size("head")
     per_group = n_seq // GROUPS
@@ -94,6 +97,100 @@
     return lax.all_to_all(result, "head", split_axis=0, concat_axis=1, tiled=True)
 
 
+def attention_kernel(block_q, counts_ref, plan_ref, mask_ref, place_ref, q_ref, k_ref, v_ref, gate_ref, out_ref):
+    tokens = q_ref.shape[0]
+    group_tok = tokens // GROUPS
+    factor = math.log2(math.e) / math.sqrt(HEAD_DIM)
+    head = place_ref[0]
+    busy = place_ref[1]
+
+    @pl.when(busy == 1)
+    def _():
+        gates = gate_ref[:, pl.ds(pl.multiple_of(head * HEAD_DIM, HEAD_DIM), HEAD_DIM)]
+        level = lax.broadcasted_iota(jnp.int32, (LEVELS, HEAD_DIM), 0)
+        for c in range(GROUPS):
+            width = (c + 1) * group_tok
+            column = lax.broadcasted_iota(jnp.int32, (1, group_tok), 1)
+            limits = [counts_ref[d] * mask_ref[c, d] for d in range(c + 1)]
+            allowed = jnp.concatenate([column < limits[d] for d in range(c + 1)], axis=1)
+            gate = jnp.sum(jnp.where(level == plan_ref[c], gates, jnp.float32(0.0)), axis=0, keepdims=True)
+
+            @pl.loop(0, group_tok // block_q)
+            def _(step):
+                row = pl.multiple_of(c * group_tok + step * block_q, block_q)
+                scores = lax.dot_general(
+                    q_ref[pl.ds(row, block_q), :],
+                    k_ref[:width, :],
+                    (((1,), (1,)), ((), ())),
+                    preferred_element_type=jnp.float32,
+                )
+                scores = jnp.where(allowed, scores, jnp.float32(-1e30))
+                top = jnp.max(scores, axis=1, keepdims=True)
+                weights = jnp.exp2(scores * factor - top * factor)
+                total = jnp.sum(weights, axis=1, keepdims=True)
+                mixed = jnp.dot(
+                    weights.astype(jnp.bfloat16), v_ref[:width, :], preferred_element_type=jnp.float32
+                )
+                position = step * block_q + lax.broadcasted_iota(jnp.int32, (block_q, 1), 0)
+                mixed = mixed / total * gate
+                out_ref[pl.ds(row, block_q), :] = jnp.where(
+                    position < counts_ref[c], mixed, jnp.float32(0.0)
+                ).astype(jnp.bfloat16)
+
+    @pl.when(busy == 0)
+    def _():
+        out_ref[...] = jnp.zeros_like(out_ref)
+
+
+def attention(q, k, v, counts, plan, group_mask, place, gate_table):
+    tokens = q.shape[0]
+    smem = pl.BlockSpec(memory_space=pltpu.SMEM)
+    vmem = pl.BlockSpec(memory_space=pltpu.VMEM)
+    return pl.pallas_call(
+        functools.partial(attention_kernel, 256),
+        out_shape=jax.ShapeDtypeStruct((tokens, HEAD_DIM), jnp.bfloat16),
+        in_specs=[smem, smem, smem, smem, vmem, vmem, vmem, vmem],
+        out_specs=vmem,
+        compiler_params=pltpu.CompilerParams(vmem_limit_bytes=40 * 1024 * 1024),
+    )(counts, plan, group_mask, place, q, k, v, gate_table)
+
+
+def head_each(queries, keys, values, counts, plan, group_mask, gate_table):
+    axes = ("seq", "head")
+    n_dev = lax.axis_size("seq") * lax.axis_size("head")
+    local = queries.shape[0]
+    heads = queries.shape[1] // HEAD_DIM
+    parts = math.gcd(heads, n_dev)
+    held, slots = heads // parts, n_dev // parts
+    index = lax.axis_index("seq") * lax.axis_size("head") + lax.axis_index("head")
+    lane = index % slots
+    busy = (lane < held).astype(jnp.int32)
+    head = jnp.minimum(index // slots * held + lane, heads - 1)
+    place = jnp.stack([head, busy]).astype(jnp.int32)
+
+    def by_slot(x):
+        x = jnp.transpose(x.reshape(local, parts, held, HEAD_DIM), (1, 2, 0, 3))
+        return jnp.pad(x, ((0, 0), (0, slots - held), (0, 0), (0, 0)))
+
+    sent = jnp.stack([by_slot(queries), by_slot(keys), by_slot(values)], axis=2)
+    sent = sent.reshape(n_dev, 3, local, HEAD_DIM)
+    got = lax.all_to_all(sent, axes, split_axis=0, concat_axis=0, tiled=True)
+    q, k, v = (got[:, i].reshape(n_dev * local, HEAD_DIM) for i in range(3))
+    result = attention(q, k, v, counts, plan, group_mask, place, gate_table)
+    back = lax.all_to_all(
+        result.reshape(n_dev, local, HEAD_DIM), axes, split_axis=0, concat_axis=0, tiled=True
+    )
+    back = back.reshape(parts, slots, local, HEAD_DIM)[:, :held]
+    return jnp.transpose(back, (2, 0, 1, 3)).reshape(local, heads * HEAD_DIM)
+
+
+def on_device(queries, keys, values, counts, plan, group_mask, gate_table):
+    n_dev = lax.axis_size("seq") * lax.axis_size("head")
+    heads = queries.shape[1] // HEAD_DIM
+    plan_of = head_each if heads <= n_dev <= 2 * heads else gathered
+    return plan_of(queries, keys, values, counts, plan, group_mask, gate_table)
+
+
 def solution(mesh):
     in_specs = (
         P(("seq", "head"), None),

time: 182 us -> 78.5 us (0.43); the launches traced: 180 us -> 78.2 us
  waiting for transfers between devices: 83.1 us -> 36.7 us
  local copies, waits for them, and re-layouts: 27.5 us -> 5.84 us
  matrix products: 17.8 us -> 0 us
  between operations: 13.6 us -> 0.19 us
  blocking collectives: 27 us -> 19.9 us
  Pallas kernels: 0 us -> 7.07 us
  other arithmetic: 7.35 us -> 1.4 us
  starting transfers between devices: 3.51 us -> 7.1 us
    all_gather x2 -> x0, waiting for transfers between devices: 83.1 us -> none  [the longest x1 42.7 us: attend(): k_piece = lax.all_gather(k_local, 'seq', axis=0, tiled=True)]
    all_to_all x1, waiting for transfers between devices: 0.01 us -> 36.7 us  [head_each(): got = lax.all_to_all(sent, axes, split_axis=0, concat_axis=0, tiled=True)]
    dot_general x3 -> x0, matrix products: 17.8 us -> none  [the longest x1 10 us: attend(): jnp.einsum('hqk,khd->hqd', rounded, v_three, preferred_element_type=jnp.f...]
    all_gather x2 -> x0, local copies, waits for them, and re-layouts: 17.4 us -> none  [the longest x1 8.7 us: attend(): v_piece = lax.all_gather(v_local, 'seq', axis=0, tiled=True)]
    all_to_all x3 -> x1, blocking collectives: 27 us -> 19.9 us  [head_each(): lax.all_to_all(result.reshape(n_dev, local, HEAD_DIM), axes, split_axis=0...]
    reduce_sum x4 -> x0, other arithmetic: 7.07 us -> none  [the longest x1 3.78 us: attend(): total = jnp.sum(weights, axis=2)]
    pallas_call x0 -> x1, Pallas kernels: none -> 7.07 us  [attention(): pl.pallas_call(functools.partial(attention_kernel, 256), out_shape=jax.Sh...]
    unnamed x6 -> x12, local copies, waits for them, and re-layouts: 4.56 us -> 0.02 us
  transfers between devices with their start and end apart: 3 -> 1, of which waited for: 2 -> 1; matrix products, arithmetic and copies ran while one was open for 15% -> 0% of each run, Pallas kernels for 0% -> 0%
where the time goes in v1:
time: 78.5 us; the launch traced here: 78.2 us
  waiting for transfers between devices  36.7 us (47%)
  blocking collectives  19.9 us (25%)
  starting transfers between devices  7.1 us (9%)
  Pallas kernels  7.07 us (9%)
  local copies, waits for them, and re-layouts  5.84 us (7%)
  other arithmetic  1.4 us (2%)
    all_to_all x1, waiting for transfers between devices, head_each(): got = lax.all_to_all(sent, axes, split_axis=0, concat_axis=0, tiled=True)  36.7 us
    all_to_all x1, blocking collectives, head_each(): lax.all_to_all(result.reshape(n_dev, local, HEAD_DIM), axes, split_axis=0...  19.9 us
    all_to_all x1, starting transfers between devices, head_each(): got = lax.all_to_all(sent, axes, split_axis=0, concat_axis=0, tiled=True)  7.1 us
    pallas_call x1, Pallas kernels, attention(): pl.pallas_call(functools.partial(attention_kernel, 256), out_shape=jax.Sh...  7.07 us
    reshape x3, local copies, waits for them, and re-layouts, by_slot(): x = jnp.transpose(x.reshape(local, parts, held, HEAD_DIM), (1, 2, 0, 3))  2.83 us
  transfers between devices with their start and end apart: 1, of which 1 were waited for; matrix products, arithmetic and copies ran while one was open for 0% of the time, Pallas kernels for 0%

profile of v1, /device:TPU:1, one launch (start us, length us, event | category | flops | bytes accessed | tf_op | source)
XLA Modules:
  0.0 78.2 jit_solution(11332730963876233219)
XLA Ops:
  0.0 0.0 copy-start.4
  0.0 1.7 %reshape.25 = bf16[64,8,3,128]{3,2,1,0:T(4,128)(2,1)S(1)} reshape(bf16[64,3072]{1,0:T(8,128)(2,1)} %param.7) | data formatting | bytes 786432 | tf_op jit(solution)/shard_map/reshape | solution.py:172
  1.7 0.2 pad.10
  1.9 0.2 copy.16
  2.2 0.0 copy-done.4
  2.2 0.0 copy-start.5
  2.2 0.6 reshape.26
  2.7 0.2 pad.11
  3.0 0.2 copy.17
  3.2 0.0 copy-done.5
  3.2 0.6 reshape.27
  3.7 0.2 pad.12
  4.0 0.2 copy.18
  4.2 1.3 %pad_maximum_fusion = bf16[32,3,64,128]{3,2,1,0:T(8,128)(2,1)} fusion(bf16[32,1,64,128]{3,2,1,0:T(8,128)(2,1)S(1)} %copy.18, bf16[32,1,64,128]{3,2,1,0:T(8,128)(2,1)S(1)} %copy.17, bf16[32,1,64,128]{3,2,1,0:T(8,128)(2,1)S(1)} %copy.16), kind=kLoop, calls=%fused_computation | loop fusion | flops 1572864 | bytes 3145728 | tf_op jit(solution)/shard_map/stack | solution.py:175
  5.5 7.1 %all-to-all-start = ((bf16[32,3,64,128]{3,2,1,0:T(8,128)(2,1)}), bf16[32,3,64,128]{3,2,1,0:T(8,128)(2,1)S(1)}, u32[]{:S(2)}, u32[]{:S(2)}) async-start(bf16[32,3,64,128]{3,2,1,0:T(8,128)(2,1)} %pad_maximum_fusion), calls=%async_computation | async-start | bytes 3145728 | tf_op jit(solution)/shard_map/all_to_all | solution.py:177
  12.6 0.1 pad_add_fusion.place_ref
  12.7 0.0 copy-start
  12.7 0.0 copy-start.1
  12.7 0.0 copy-start.2
  12.7 0.0 copy-start.3
  12.7 36.7 %all-to-all-done = bf16[32,3,64,128]{3,2,1,0:T(8,128)(2,1)S(1)} async-done(((bf16[32,3,64,128]{3,2,1,0:T(8,128)(2,1)}), bf16[32,3,64,128]{3,2,1,0:T(8,128)(2,1)S(1)}, u32[]{:S(2)}, u32[]{:S(2)}) %all-to-all-start) | async-done | bytes 1572896 | tf_op jit(solution)/shard_map/all_to_all | solution.py:177
  49.5 0.1 fusion
  49.6 0.0 copy-done
  49.6 0.0 copy-done.1
  49.6 0.0 copy-done.2
  49.6 0.0 copy-done.3
  49.6 7.1 %shard_map.73 = bf16[2048,128]{1,0:T(8,128)(2,1)S(1)} custom-call(s32[4]{0:T(128)S(1)} %copy-done.2, s32[4]{0:T(128)S(1)} %copy-done.3, s32[4,4]{1,0:T(4,128)S(1)} %copy-done.1, s32[2]{0:T(128)S(1)} %pad_add_fusion.place_ref, bf16[2048,128]{1,0:T(8,128)(2,1)S(1)} %bitcast.18, bf16[2048,128]{1,0:T(8,128)(2,1)S(1)} %bitcast.17, ...), custom_call_target="tpu_custom_call" | custom-call | tf_op jit(solution)/shard_map/pallas_call | solution.py:149
  56.7 19.9 %all_to_all.10 = bf16[32,64,128]{2,1,0:T(8,128)(2,1)S(1)} all-to-all(bf16[32,64,128]{2,1,0:T(8,128)(2,1)S(1)} %bitcast.15), channel_id=1, replica_groups=mesh['seq'=16,'head'=2] {'seq','head'}, dimensions={0} | all-to-all | bytes 1048576 | tf_op jit(solution)/shard_map/all_to_all | solution.py:180
  76.6 0.3 copy.19
  76.9 0.2 slice_bitcast_fusion
  77.1 1.1 %reshape.30 = bf16[64,3072]{1,0:T(8,128)(2,1)} reshape(bf16[64,8,3,128]{3,2,1,0:T(4,128)(2,1)S(1)} %slice_bitcast_fusion) | data formatting | bytes 786432 | tf_op jit(solution)/shard_map/reshape | solution.py:184
Async XLA Ops:
  0.0 2.2 %copy-start.4 = (bf16[64,3072]{1,0:T(8,128)(2,1)S(1)}, bf16[64,3072]{1,0:T(8,128)(2,1)}, u32[]{:S(2)}) copy-start(bf16[64,3072]{1,0:T(8,128)(2,1)} %param.8) | copy-start | bytes 1179652
  2.2 1.0 %copy-start.5 = (bf16[64,3072]{1,0:T(8,128)(2,1)S(1)}, bf16[64,3072]{1,0:T(8,128)(2,1)}, u32[]{:S(2)}) copy-start(bf16[64,3072]{1,0:T(8,128)(2,1)} %param.9) | copy-start | bytes 1179652
  5.5 44.0 %all-to-all-start = ((bf16[32,3,64,128]{3,2,1,0:T(8,128)(2,1)}), bf16[32,3,64,128]{3,2,1,0:T(8,128)(2,1)S(1)}, u32[]{:S(2)}, u32[]{:S(2)}) async-start(bf16[32,3,64,128]{3,2,1,0:T(8,128)(2,1)} %pad_maximum_fusion), calls=%async_computation | async-start | bytes 3145728 | tf_op jit(solution)/shard_map/all_to_all | solution.py:177
  12.7 36.9 %copy-start = (f32[8,3072]{1,0:T(8,128)S(1)}, f32[8,3072]{1,0:T(8,128)}, u32[]{:S(2)}) copy-start(f32[8,3072]{1,0:T(8,128)} %gate_ref.1) | copy-start | bytes 294916
  12.7 36.9 %copy-start.1 = (s32[4,4]{1,0:T(4,128)S(1)}, s32[4,4]{1,0:T(4,128)}, u32[]{:S(2)}) copy-start(s32[4,4]{1,0:T(4,128)} %mask_ref.1) | copy-start | bytes 196
  12.7 36.9 %copy-start.2 = (s32[4]{0:T(128)S(1)}, s32[4]{0:T(128)}, u32[]{:S(2)}) copy-start(s32[4]{0:T(128)} %counts_ref.1) | copy-start | bytes 52
  12.7 36.9 %copy-start.3 = (s32[4]{0:T(128)S(1)}, s32[4]{0:T(128)}, u32[]{:S(2)}) copy-start(s32[4]{0:T(128)} %plan_ref.1) | copy-start | bytes 52

commit v2 on v1

--- a/solution.py
+++ b/solution.py
@@ -97,9 +97,31 @@
     return lax.all_to_all(result, "head", split_axis=0, concat_axis=1, tiled=True)
 
 
-def attention_kernel(block_q, counts_ref, plan_ref, mask_ref, place_ref, q_ref, k_ref, v_ref, gate_ref, out_ref):
-    tokens = q_ref.shape[0]
-    group_tok = tokens // GROUPS
+def pack_kernel(parts, held, q_ref, k_ref, v_ref, out_ref):
+    slots = out_ref.shape[0] // parts
+    for p in range(parts):
+        for s in range(slots):
+            for i, ref in enumerate((q_ref, k_ref, v_ref)):
+                if s < held:
+                    h = p * held + s
+                    out_ref[p * slots + s, i] = ref[:, h * HEAD_DIM : (h + 1) * HEAD_DIM]
+                else:
+                    out_ref[p * slots + s, i] = jnp.zeros(out_ref.shape[2:], out_ref.dtype)
+
+
+def unpack_kernel(parts, held, in_ref, out_ref):
+    slots = in_ref.shape[0] // parts
+    for p in range(parts):
+        for s in range(held):
+            h = p * held + s
+            out_ref[:, h * HEAD_DIM : (h + 1) * HEAD_DIM] = in_ref[p * slots + s]
+
+
+def attention_kernel(block, counts_ref, plan_ref, mask_ref, place_ref, got_ref, gate_ref, out_ref):
+    n_dev, _, local, _ = got_ref.shape
+    per_group = n_dev // GROUPS
+    group_tok = per_group * local
+    rows = block * local
     factor = math.log2(math.e) / math.sqrt(HEAD_DIM)
     head = place_ref[0]
     busy = place_ref[1]
@@ -115,12 +137,12 @@
             allowed = jnp.concatenate([column < limits[d] for d in range(c + 1)], axis=1)
             gate = jnp.sum(jnp.where(level == plan_ref[c], gates, jnp.float32(0.0)), axis=0, keepdims=True)
 
-            @pl.loop(0, group_tok // block_q)
+            @pl.loop(0, per_group // block)
             def _(step):
-                row = pl.multiple_of(c * group_tok + step * block_q, block_q)
+                first = c * per_group + step * block
                 scores = lax.dot_general(
-                    q_ref[pl.ds(row, block_q), :],
-                    k_ref[:width, :],
+                    got_ref[pl.ds(first, block), 0].reshape(rows, HEAD_DIM),
+                    got_ref[: (c + 1) * per_group, 1].reshape(width, HEAD_DIM),
                     (((1,), (1,)), ((), ())),
                     preferred_element_type=jnp.float32,
                 )
@@ -129,37 +151,24 @@
                 weights = jnp.exp2(scores * factor - top * factor)
                 total = jnp.sum(weights, axis=1, keepdims=True)
                 mixed = jnp.dot(
-                    weights.astype(jnp.bfloat16), v_ref[:width, :], preferred_element_type=jnp.float32
+                    weights.astype(jnp.bfloat16),
+                    got_ref[: (c + 1) * per_group, 2].reshape(width, HEAD_DIM),
+                    preferred_element_type=jnp.float32,
                 )
-                position = step * block_q + lax.broadcasted_iota(jnp.int32, (block_q, 1), 0)
-                mixed = mixed / total * gate
-                out_ref[pl.ds(row, block_q), :] = jnp.where(
-                    position < counts_ref[c], mixed, jnp.float32(0.0)
-                ).astype(jnp.bfloat16)
+                position = step * rows + lax.broadcasted_iota(jnp.int32, (rows, 1), 0)
+                mixed = jnp.where(position < counts_ref[c], mixed / total * gate, jnp.float32(0.0))
+                out_ref[pl.ds(first, block)] = mixed.astype(jnp.bfloat16).reshape(block, local, HEAD_DIM)
 
     @pl.when(busy == 0)
     def _():
         out_ref[...] = jnp.zeros_like(out_ref)
 
 
-def attention(q, k, v, counts, plan, group_mask, place, gate_table):
-    tokens = q.shape[0]
-    smem = pl.BlockSpec(memory_space=pltpu.SMEM)
-    vmem = pl.BlockSpec(memory_space=pltpu.VMEM)
-    return pl.pallas_call(
-        functools.partial(attention_kernel, 256),
-        out_shape=jax.ShapeDtypeStruct((tokens, HEAD_DIM), jnp.bfloat16),
-        in_specs=[smem, smem, smem, smem, vmem, vmem, vmem, vmem],
-        out_specs=vmem,
-        compiler_params=pltpu.CompilerParams(vmem_limit_bytes=40 * 1024 * 1024),
-    )(counts, plan, group_mask, place, q, k, v, gate_table)
-
-
 def head_each(queries, keys, values, counts, plan, group_mask, gate_table):
     axes = ("seq", "head")
     n_dev = lax.axis_size("seq") * lax.axis_size("head")
-    local = queries.shape[0]
-    heads = queries.shape[1] // HEAD_DIM
+    local, feat = queries.shape
+    heads = feat // HEAD_DIM
     parts = math.gcd(heads, n_dev)
     held, slots = heads // parts, n_dev // parts
     index = lax.axis_index("seq") * lax.axis_size("head") + lax.axis_index("head")
@@ -167,21 +176,35 @@
     busy = (lane < held).astype(jnp.int32)
     head = jnp.minimum(index // slots * held + lane, heads - 1)
     place = jnp.stack([head, busy]).astype(jnp.int32)
-
-    def by_slot(x):
-        x = jnp.transpose(x.reshape(local, parts, held, HEAD_DIM), (1, 2, 0, 3))
-        return jnp.pad(x, ((0, 0), (0, slots - held), (0, 0), (0, 0)))
-
-    sent = jnp.stack([by_slot(queries), by_slot(keys), by_slot(values)], axis=2)
-    sent = sent.reshape(n_dev, 3, local, HEAD_DIM)
+    smem = pl.BlockSpec(memory_space=pltpu.SMEM)
+    vmem = pl.BlockSpec(memory_space=pltpu.VMEM)
+
+    sent = pl.pallas_call(
+        functools.partial(pack_kernel, parts, held),
+        out_shape=jax.ShapeDtypeStruct((n_dev, 3, local, HEAD_DIM), jnp.bfloat16),
+        in_specs=[vmem] * 3,
+        out_specs=vmem,
+        compiler_params=pltpu.CompilerParams(vmem_limit_bytes=16 * 1024 * 1024),
+        name="pack",
+    )(queries, keys, values)
     got = lax.all_to_all(sent, axes, split_axis=0, concat_axis=0, tiled=True)
-    q, k, v = (got[:, i].reshape(n_dev * local, HEAD_DIM) for i in range(3))
-    result = attention(q, k, v, counts, plan, group_mask, place, gate_table)
-    back = lax.all_to_all(
-        result.reshape(n_dev, local, HEAD_DIM), axes, split_axis=0, concat_axis=0, tiled=True
-    )
-    back = back.reshape(parts, slots, local, HEAD_DIM)[:, :held]
-    return jnp.transpose(back, (2, 0, 1, 3)).reshape(local, heads * HEAD_DIM)
+    result = pl.pallas_call(
+        functools.partial(attention_kernel, max(1, 256 // local)),
+        out_shape=jax.ShapeDtypeStruct((n_dev, local, HEAD_DIM), jnp.bfloat16),
+        in_specs=[smem, smem, smem, smem, vmem, vmem],
+        out_specs=vmem,
+        compiler_params=pltpu.CompilerParams(vmem_limit_bytes=40 * 1024 * 1024),
+        name="attention",
+    )(counts, plan, group_mask, place, got, gate_table)
+    back = lax.all_to_all(result, axes, split_axis=0, concat_axis=0, tiled=True)
+    return pl.pallas_call(
+        functools.partial(unpack_kernel, parts, held),
+        out_shape=jax.ShapeDtypeStruct((local, feat), jnp.bfloat16),
+        in_specs=[vmem],
+        out_specs=vmem,
+        compiler_params=pltpu.CompilerParams(vmem_limit_bytes=16 * 1024 * 1024),
+        name="unpack",
+    )(back)
 
 
 def on_device(queries, keys, values, counts, plan, group_mask, gate_table):

time: 78.5 us -> 76.5 us (0.975)
  local copies, waits for them, and re-layouts: 5.84 us -> 3 us
  Pallas kernels: 7.07 us -> 9.28 us
  other arithmetic: 1.4 us -> 0.08 us
    reshape x4 -> x0, local copies, waits for them, and re-layouts: 3.91 us -> none  [the longest x3 2.83 us: by_slot(): x = jnp.transpose(x.reshape(local, parts, held, HEAD_DIM), (1, 2, 0, 3))]
    unnamed x12 -> x14, local copies, waits for them, and re-layouts: 0.02 us -> 3 us
    pallas_call x1 -> x3, Pallas kernels: 7.07 us -> 9.28 us  [the longest x1 7.07 us: head_each(): pl.pallas_call(functools.partial(attention_kernel, max(1, 256 // local)),...]
    another operation x1 -> x0, other arithmetic: 1.32 us -> none  [head_each(): sent = jnp.stack([by_slot(queries), by_slot(keys), by_slot(values)], axis=2)]
where the time goes in v2:
time: 76.5 us; the launch traced here: 76.1 us
  waiting for transfers between devices  36.8 us (48%)
  blocking collectives  19.9 us (26%)
  Pallas kernels  9.28 us (12%)
  starting transfers between devices  7.1 us (9%)
  local copies, waits for them, and re-layouts  3 us (4%)
    all_to_all x1, waiting for transfers between devices, head_each(): got = lax.all_to_all(sent, axes, split_axis=0, concat_axis=0, tiled=True)  36.8 us
    all_to_all x1, blocking collectives, head_each(): back = lax.all_to_all(result, axes, split_axis=0, concat_axis=0, tiled=True)  19.9 us
    all_to_all x1, starting transfers between devices, head_each(): got = lax.all_to_all(sent, axes, split_axis=0, concat_axis=0, tiled=True)  7.1 us
    pallas_call x1, Pallas kernels, head_each(): pl.pallas_call(functools.partial(attention_kernel, max(1, 256 // local)),...  7.07 us
    unnamed x14, local copies, waits for them, and re-layouts  3 us
  transfers between devices with their start and end apart: 1, of which 1 were waited for; matrix products, arithmetic and copies ran while one was open for 0% of the time, Pallas kernels for 0%

profile of v2, /device:TPU:1, one launch (start us, length us, event | category | flops | bytes accessed | tf_op | source)
XLA Modules:
  0.0 76.1 jit_solution(6570179138611170597)
XLA Ops:
  0.0 0.0 copy-start
  0.0 1.0 %copy-done = bf16[64,3072]{1,0:T(8,128)(2,1)S(1)} copy-done((bf16[64,3072]{1,0:T(8,128)(2,1)S(1)}, bf16[64,3072]{1,0:T(8,128)(2,1)}, u32[]{:S(2)}) %copy-start) | copy-done | bytes 393240
  1.0 0.0 copy-start.1
  1.0 1.0 %copy-done.1 = bf16[64,3072]{1,0:T(8,128)(2,1)S(1)} copy-done((bf16[64,3072]{1,0:T(8,128)(2,1)S(1)}, bf16[64,3072]{1,0:T(8,128)(2,1)}, u32[]{:S(2)}) %copy-start.1) | copy-done | bytes 393240
  2.0 0.0 copy-start.2
  2.0 1.0 %copy-done.2 = bf16[64,3072]{1,0:T(8,128)(2,1)S(1)} copy-done((bf16[64,3072]{1,0:T(8,128)(2,1)S(1)}, bf16[64,3072]{1,0:T(8,128)(2,1)}, u32[]{:S(2)}) %copy-start.2) | copy-done | bytes 393240
  3.0 1.4 %pack.1 = bf16[32,3,64,128]{3,2,1,0:T(8,128)(2,1)} custom-call(bf16[64,3072]{1,0:T(8,128)(2,1)S(1)} %copy-done, bf16[64,3072]{1,0:T(8,128)(2,1)S(1)} %copy-done.1, bf16[64,3072]{1,0:T(8,128)(2,1)S(1)} %copy-done.2), custom_call_target="tpu_custom_call" | custom-call | tf_op jit(solution)/shard_map/pack/pallas_call | solution.py:182
  4.4 0.0 copy-start.3
  4.4 0.0 copy-start.4
  4.4 0.0 copy-start.5
  4.4 0.0 copy-start.6
  4.4 7.1 %all-to-all-start = ((bf16[32,3,64,128]{3,2,1,0:T(8,128)(2,1)}), bf16[32,3,64,128]{3,2,1,0:T(8,128)(2,1)S(1)}, u32[]{:S(2)}, u32[]{:S(2)}) async-start(bf16[32,3,64,128]{3,2,1,0:T(8,128)(2,1)} %pack.1), calls=%async_computation | async-start | bytes 3145728 | tf_op jit(solution)/shard_map/all_to_all | solution.py:190
  11.5 0.1 pad_add_fusion.place_ref
  11.6 36.8 %all-to-all-done.got_ref = bf16[32,3,64,128]{3,2,1,0:T(8,128)(2,1)S(1)} async-done(((bf16[32,3,64,128]{3,2,1,0:T(8,128)(2,1)}), bf16[32,3,64,128]{3,2,1,0:T(8,128)(2,1)S(1)}, u32[]{:S(2)}, u32[]{:S(2)}) %all-to-all-start) | async-done | bytes 1572896 | tf_op jit(solution)/shard_map/all_to_all | solution.py:190
  48.4 0.0 copy-done.3
  48.4 0.0 copy-done.4
  48.4 0.0 copy-done.5
  48.4 0.0 copy-done.6
  48.4 7.1 %attention.1 = bf16[32,64,128]{2,1,0:T(8,128)(2,1)S(1)} custom-call(s32[4]{0:T(128)S(1)} %copy-done.5, s32[4]{0:T(128)S(1)} %copy-done.6, s32[4,4]{1,0:T(4,128)S(1)} %copy-done.4, s32[2]{0:T(128)S(1)} %pad_add_fusion.place_ref, bf16[32,3,64,128]{3,2,1,0:T(8,128)(2,1)S(1)} %all-to-all-done.got_ref, f32[8,3072]{1,0:T(8,128)S(1)} %copy-done.3), custom_call_target="tpu_custom_call" | custom-call | tf_op jit(solution)/shard_map/attention/pallas_call | solution.py:191
  55.5 19.9 %all_to_all.10.in_ref = bf16[32,64,128]{2,1,0:T(8,128)(2,1)S(1)} all-to-all(bf16[32,64,128]{2,1,0:T(8,128)(2,1)S(1)} %attention.1), channel_id=1, replica_groups=mesh['seq'=16,'head'=2] {'seq','head'}, dimensions={0} | all-to-all | bytes 1048576 | tf_op jit(solution)/shard_map/all_to_all | solution.py:199
  75.3 0.8 %unpack.1 = bf16[64,3072]{1,0:T(8,128)(2,1)} custom-call(bf16[32,64,128]{2,1,0:T(8,128)(2,1)S(1)} %all_to_all.10.in_ref), custom_call_target="tpu_custom_call" | custom-call | tf_op jit(solution)/shard_map/unpack/pallas_call | solution.py:200
Async XLA Ops:
  0.0 1.0 %copy-start = (bf16[64,3072]{1,0:T(8,128)(2,1)S(1)}, bf16[64,3072]{1,0:T(8,128)(2,1)}, u32[]{:S(2)}) copy-start(bf16[64,3072]{1,0:T(8,128)(2,1)} %q_ref.1) | copy-start | bytes 1179652
  1.0 1.0 %copy-start.1 = (bf16[64,3072]{1,0:T(8,128)(2,1)S(1)}, bf16[64,3072]{1,0:T(8,128)(2,1)}, u32[]{:S(2)}) copy-start(bf16[64,3072]{1,0:T(8,128)(2,1)} %k_ref.1) | copy-start | bytes 1179652
  2.0 1.0 %copy-start.2 = (bf16[64,3072]{1,0:T(8,128)(2,1)S(1)}, bf16[64,3072]{1,0:T(8,128)(2,1)}, u32[]{:S(2)}) copy-start(bf16[64,3072]{1,0:T(8,128)(2,1)} %v_ref.1) | copy-start | bytes 1179652
  4.4 44.0 %copy-start.3 = (f32[8,3072]{1,0:T(8,128)S(1)}, f32[8,3072]{1,0:T(8,128)}, u32[]{:S(2)}) copy-start(f32[8,3072]{1,0:T(8,128)} %gate_ref.1) | copy-start | bytes 294916
  4.4 44.0 %copy-start.4 = (s32[4,4]{1,0:T(4,128)S(1)}, s32[4,4]{1,0:T(4,128)}, u32[]{:S(2)}) copy-start(s32[4,4]{1,0:T(4,128)} %mask_ref.1) | copy-start | bytes 196
  4.4 44.0 %copy-start.5 = (s32[4]{0:T(128)S(1)}, s32[4]{0:T(128)}, u32[]{:S(2)}) copy-start(s32[4]{0:T(128)} %counts_ref.1) | copy-start | bytes 52
  4.4 44.0 %copy-start.6 = (s32[4]{0:T(128)S(1)}, s32[4]{0:T(128)}, u32[]{:S(2)}) copy-start(s32[4]{0:T(128)} %plan_ref.1) | copy-start | bytes 52
  4.4 44.0 %all-to-all-start = ((bf16[32,3,64,128]{3,2,1,0:T(8,128)(2,1)}), bf16[32,3,64,128]{3,2,1,0:T(8,128)(2,1)S(1)}, u32[]{:S(2)}, u32[]{:S(2)}) async-start(bf16[32,3,64,128]{3,2,1,0:T(8,128)(2,1)} %pack.1), calls=%async_computation | async-start | bytes 3145728 | tf_op jit(solution)/shard_map/all_to_all | solution.py:190

commit v3 on v2

--- a/solution.py
+++ b/solution.py
@@ -97,16 +97,14 @@
     return lax.all_to_all(result, "head", split_axis=0, concat_axis=1, tiled=True)
 
 
-def pack_kernel(parts, held, q_ref, k_ref, v_ref, out_ref):
-    slots = out_ref.shape[0] // parts
-    for p in range(parts):
-        for s in range(slots):
-            for i, ref in enumerate((q_ref, k_ref, v_ref)):
-                if s < held:
-                    h = p * held + s
-                    out_ref[p * slots + s, i] = ref[:, h * HEAD_DIM : (h + 1) * HEAD_DIM]
-                else:
-                    out_ref[p * slots + s, i] = jnp.zeros(out_ref.shape[2:], out_ref.dtype)
+def pack_kernel(held, slots, place_ref, q_ref, k_ref, v_ref, *out_refs):
+    n_dev = len(out_refs)
+    for step, out_ref in enumerate(out_refs):
+        dest = lax.rem(place_ref[2] + step, n_dev)
+        head = lax.div(dest, slots) * held + jnp.minimum(lax.rem(dest, slots), held - 1)
+        columns = pl.ds(pl.multiple_of(head * HEAD_DIM, HEAD_DIM), HEAD_DIM)
+        for i, ref in enumerate((q_ref, k_ref, v_ref)):
+            out_ref[i] = ref[:, columns]
 
 
 def unpack_kernel(parts, held, in_ref, out_ref):
@@ -117,7 +115,8 @@
             out_ref[:, h * HEAD_DIM : (h + 1) * HEAD_DIM] = in_ref[p * slots + s]
 
 
-def attention_kernel(block, counts_ref, plan_ref, mask_ref, place_ref, got_ref, gate_ref, out_ref):
+def attention_kernel(block, counts_ref, plan_ref, mask_ref, place_ref, gate_ref, *refs):
+    *in_refs, out_ref, got_ref = refs
     n_dev, _, local, _ = got_ref.shape
     per_group = n_dev // GROUPS
     group_tok = per_group * local
@@ -128,6 +127,8 @@
 
     @pl.when(busy == 1)
     def _():
+        for step, in_ref in enumerate(in_refs):
+            got_ref[lax.rem(place_ref[2] + n_dev - step, n_dev)] = in_ref[...]
         gates = gate_ref[:, pl.ds(pl.multiple_of(head * HEAD_DIM, HEAD_DIM), HEAD_DIM)]
         level = lax.broadcasted_iota(jnp.int32, (LEVELS, HEAD_DIM), 0)
         for c in range(GROUPS):
@@ -175,27 +176,35 @@
     lane = index % slots
     busy = (lane < held).astype(jnp.int32)
     head = jnp.minimum(index // slots * held + lane, heads - 1)
-    place = jnp.stack([head, busy]).astype(jnp.int32)
+    place = jnp.stack([head, busy, index]).astype(jnp.int32)
     smem = pl.BlockSpec(memory_space=pltpu.SMEM)
     vmem = pl.BlockSpec(memory_space=pltpu.VMEM)
 
+    piece = jax.ShapeDtypeStruct((3, local, HEAD_DIM), jnp.bfloat16)
     sent = pl.pallas_call(
-        functools.partial(pack_kernel, parts, held),
-        out_shape=jax.ShapeDtypeStruct((n_dev, 3, local, HEAD_DIM), jnp.bfloat16),
-        in_specs=[vmem] * 3,
-        out_specs=vmem,
+        functools.partial(pack_kernel, held, slots),
+        out_shape=[piece] * n_dev,
+        in_specs=[smem] + [vmem] * 3,
+        out_specs=[vmem] * n_dev,
         compiler_params=pltpu.CompilerParams(vmem_limit_bytes=16 * 1024 * 1024),
         name="pack",
-    )(queries, keys, values)
-    got = lax.all_to_all(sent, axes, split_axis=0, concat_axis=0, tiled=True)
+    )(place, queries, keys, values)
+    got = [sent[0]] * n_dev
+    bits = (n_dev - 1).bit_length()
+    order = sorted(range(1, n_dev), key=lambda step: format(step, f"0{bits}b")[::-1])
+    for step in order:
+        pairs = [(d, (d + step) % n_dev) for d in range(n_dev)]
+        pairs = [(d, e) for d, e in pairs if e % slots < held]
+        got[step] = lax.ppermute(sent[step], axes, pairs)
     result = pl.pallas_call(
         functools.partial(attention_kernel, max(1, 256 // local)),
         out_shape=jax.ShapeDtypeStruct((n_dev, local, HEAD_DIM), jnp.bfloat16),
-        in_specs=[smem, smem, smem, smem, vmem, vmem],
+        in_specs=[smem, smem, smem, smem, vmem] + [vmem] * n_dev,
         out_specs=vmem,
+        scratch_shapes=[pltpu.VMEM((n_dev, 3, local, HEAD_DIM), jnp.bfloat16)],
         compiler_params=pltpu.CompilerParams(vmem_limit_bytes=40 * 1024 * 1024),
         name="attention",
-    )(counts, plan, group_mask, place, got, gate_table)
+    )(counts, plan, group_mask, place, gate_table, *got)
     back = lax.all_to_all(result, axes, split_axis=0, concat_axis=0, tiled=True)
     return pl.pallas_call(
         functools.partial(unpack_kernel, parts, held),

time: 76.5 us -> 137 us (1.79)
  starting transfers between devices: 7.1 us -> 101 us
  waiting for transfers between devices: 36.8 us -> 3.36 us
  blocking collectives: 19.9 us -> 18.1 us
    ppermute x0 -> x31, starting transfers between devices: none -> 101 us  [head_each(): got[step] = lax.ppermute(sent[step], axes, pairs)]
    all_to_all x1 -> x0, waiting for transfers between devices: 36.8 us -> none  [head_each(): got = lax.all_to_all(sent, axes, split_axis=0, concat_axis=0, tiled=True)]
    all_to_all x1 -> x0, starting transfers between devices: 7.1 us -> none  [head_each(): got = lax.all_to_all(sent, axes, split_axis=0, concat_axis=0, tiled=True)]
    ppermute x0 -> x31, waiting for transfers between devices: none -> 3.36 us  [head_each(): got[step] = lax.ppermute(sent[step], axes, pairs)]
    all_to_all x1, blocking collectives: 19.9 us -> 18.1 us  [head_each(): back = lax.all_to_all(result, axes, split_axis=0, concat_axis=0, tiled=True)]
  transfers between devices with their start and end apart: 1 -> 31, of which waited for: 1 -> 1; matrix products, arithmetic and copies ran while one was open for 0% -> 0% of each run, Pallas kernels for 0% -> 0%
where the time goes in v3:
time: 137 us; the launch traced here: 136 us
  starting transfers between devices  101 us (74%)
  blocking collectives  18.1 us (13%)
  Pallas kernels  9.21 us (7%)
  waiting for transfers between devices  3.36 us (2%)
  local copies, waits for them, and re-layouts  3.01 us (2%)
    ppermute x31, starting transfers between devices, head_each(): got[step] = lax.ppermute(sent[step], axes, pairs)  101 us
    all_to_all x1, blocking collectives, head_each(): back = lax.all_to_all(result, axes, split_axis=0, concat_axis=0, tiled=True)  18.1 us
    pallas_call x1, Pallas kernels, head_each(): pl.pallas_call(functools.partial(attention_kernel, max(1, 256 // local)),...  7.42 us
    ppermute x31, waiting for transfers between devices, head_each(): got[step] = lax.ppermute(sent[step], axes, pairs)  3.36 us
    unnamed x14, local copies, waits for them, and re-layouts  3.01 us
  transfers between devices with their start and end apart: 31, of which 1 were waited for; matrix products, arithmetic and copies ran while one was open for 0% of the time, Pallas kernels for 0%

profile of v3, /device:TPU:1, one launch (start us, length us, event | category | flops | bytes accessed | tf_op | source)
XLA Modules:
  0.0 135.6 jit_solution(9852712704247811605)
XLA Ops:
  0.0 0.1 pad_add_fusion.place_ref
  0.1 1.0 copy-done
  1.1 1.0 copy-done.1
  2.1 1.0 copy-done.2
  3.1 1.0 pack.1
  4.1 1.3 collective-permute-start
  5.4 6.6 %collective-permute-start.1 = (bf16[3,64,128]{2,1,0:T(8,128)(2,1)S(1)}, bf16[3,64,128]{2,1,0:T(8,128)(2,1)S(1)}, u32[]{:S(2)}, u32[]{:S(2)}) collective-permute-start(bf16[3,64,128]{2,1,0:T(8,128)(2,1)S(1)} %get-tuple-element.39), channel_id=1, source_target_pairs={{0,2},{2,4},{3,5},{4,6},{6,8},{7,9},{8,10},{10,12},{11,13},{12,14}... | collective-permute-start | bytes 147464 | tf_op jit(solution)/shard_map/ppermute | solution.py:198
  12.0 1.9 %collective-permute-start.2 = (bf16[3,64,128]{2,1,0:T(8,128)(2,1)S(1)}, bf16[3,64,128]{2,1,0:T(8,128)(2,1)S(1)}, u32[]{:S(2)}, u32[]{:S(2)}) collective-permute-start(bf16[3,64,128]{2,1,0:T(8,128)(2,1)S(1)} %get-tuple-element.40), channel_id=1, source_target_pairs={{1,4},{2,5},{3,6},{5,8},{6,9},{7,10},{9,12},{10,13},{11,14},{13,16... | collective-permute-start | bytes 147464 | tf_op jit(solution)/shard_map/ppermute | solution.py:198
  13.9 3.1 %collective-permute-start.3 = (bf16[3,64,128]{2,1,0:T(8,128)(2,1)S(1)}, bf16[3,64,128]{2,1,0:T(8,128)(2,1)S(1)}, u32[]{:S(2)}, u32[]{:S(2)}) collective-permute-start(bf16[3,64,128]{2,1,0:T(8,128)(2,1)S(1)} %get-tuple-element.41), channel_id=1, source_target_pairs={{0,4},{1,5},{2,6},{4,8},{5,9},{6,10},{8,12},{9,13},{10,14},{12,16}... | collective-permute-start | bytes 147464 | tf_op jit(solution)/shard_map/ppermute | solution.py:198
  17.1 1.3 collective-permute-start.4
  18.4 0.0 collective-permute-done.refs_1_
  18.4 6.8 %collective-permute-start.5 = (bf16[3,64,128]{2,1,0:T(8,128)(2,1)S(1)}, bf16[3,64,128]{2,1,0:T(8,128)(2,1)S(1)}, u32[]{:S(2)}, u32[]{:S(2)}) collective-permute-start(bf16[3,64,128]{2,1,0:T(8,128)(2,1)S(1)} %get-tuple-element.43), channel_id=1, source_target_pairs={{0,6},{2,8},{3,9},{4,10},{6,12},{7,13},{8,14},{10,16},{11,17},{12,... | collective-permute-start | bytes 147464 | tf_op jit(solution)/shard_map/ppermute | solution.py:198
  25.2 0.0 collective-permute-done.1.refs_2_
  25.2 1.9 %collective-permute-start.6 = (bf16[3,64,128]{2,1,0:T(8,128)(2,1)S(1)}, bf16[3,64,128]{2,1,0:T(8,128)(2,1)S(1)}, u32[]{:S(2)}, u32[]{:S(2)}) collective-permute-start(bf16[3,64,128]{2,1,0:T(8,128)(2,1)S(1)} %get-tuple-element.44), channel_id=1, source_target_pairs={{1,8},{2,9},{3,10},{5,12},{6,13},{7,14},{9,16},{10,17},{11,18},{13... | collective-permute-start | bytes 147464 | tf_op jit(solution)/shard_map/ppermute | solution.py:198
  27.1 0.0 collective-permute-done.2.refs_3_
  27.2 3.2 %collective-permute-start.7 = (bf16[3,64,128]{2,1,0:T(8,128)(2,1)S(1)}, bf16[3,64,128]{2,1,0:T(8,128)(2,1)S(1)}, u32[]{:S(2)}, u32[]{:S(2)}) collective-permute-start(bf16[3,64,128]{2,1,0:T(8,128)(2,1)S(1)} %get-tuple-element.45), channel_id=1, source_target_pairs={{0,8},{1,9},{2,10},{4,12},{5,13},{6,14},{8,16},{9,17},{10,18},{12,... | collective-permute-start | bytes 147464 | tf_op jit(solution)/shard_map/ppermute | solution.py:198
  30.4 1.3 collective-permute-start.8
  31.7 0.0 collective-permute-done.4.refs_5_
  31.7 6.5 %collective-permute-start.9 = (bf16[3,64,128]{2,1,0:T(8,128)(2,1)S(1)}, bf16[3,64,128]{2,1,0:T(8,128)(2,1)S(1)}, u32[]{:S(2)}, u32[]{:S(2)}) collective-permute-start(bf16[3,64,128]{2,1,0:T(8,128)(2,1)S(1)} %get-tuple-element.47), channel_id=1, source_target_pairs={{0,10},{2,12},{3,13},{4,14},{6,16},{7,17},{8,18},{10,20},{11,21},{... | collective-permute-start | bytes 147464 | tf_op jit(solution)/shard_map/ppermute | solution.py:198
  38.2 1.9 %collective-permute-start.10 = (bf16[3,64,128]{2,1,0:T(8,128)(2,1)S(1)}, bf16[3,64,128]{2,1,0:T(8,128)(2,1)S(1)}, u32[]{:S(2)}, u32[]{:S(2)}) collective-permute-start(bf16[3,64,128]{2,1,0:T(8,128)(2,1)S(1)} %get-tuple-element.48), channel_id=1, source_target_pairs={{1,12},{2,13},{3,14},{5,16},{6,17},{7,18},{9,20},{10,21},{11,22},{... | collective-permute-start | bytes 147464 | tf_op jit(solution)/shard_map/ppermute | solution.py:198
  40.1 0.0 collective-permute-done.6.refs_7_
  40.1 4.2 %collective-permute-start.11 = (bf16[3,64,128]{2,1,0:T(8,128)(2,1)S(1)}, bf16[3,64,128]{2,1,0:T(8,128)(2,1)S(1)}, u32[]{:S(2)}, u32[]{:S(2)}) collective-permute-start(bf16[3,64,128]{2,1,0:T(8,128)(2,1)S(1)} %get-tuple-element.49), channel_id=1, source_target_pairs={{0,12},{1,13},{2,14},{4,16},{5,17},{6,18},{8,20},{9,21},{10,22},{1... | collective-permute-start | bytes 147464 | tf_op jit(solution)/shard_map/ppermute | solution.py:198
  44.3 0.0 collective-permute-done.7.refs_8_
  44.3 1.3 collective-permute-start.12
  45.6 6.6 %collective-permute-start.13 = (bf16[3,64,128]{2,1,0:T(8,128)(2,1)S(1)}, bf16[3,64,128]{2,1,0:T(8,128)(2,1)S(1)}, u32[]{:S(2)}, u32[]{:S(2)}) collective-permute-start(bf16[3,64,128]{2,1,0:T(8,128)(2,1)S(1)} %get-tuple-element.51), channel_id=1, source_target_pairs={{0,14},{2,16},{3,17},{4,18},{6,20},{7,21},{8,22},{10,24},{11,25},{... | collective-permute-start | bytes 147464 | tf_op jit(solution)/shard_map/ppermute | solution.py:198
  52.2 0.0 collective-permute-done.9.refs_10_
  52.2 1.9 %collective-permute-start.14 = (bf16[3,64,128]{2,1,0:T(8,128)(2,1)S(1)}, bf16[3,64,128]{2,1,0:T(8,128)(2,1)S(1)}, u32[]{:S(2)}, u32[]{:S(2)}) collective-permute-start(bf16[3,64,128]{2,1,0:T(8,128)(2,1)S(1)} %get-tuple-element.52), channel_id=1, source_target_pairs={{1,16},{2,17},{3,18},{5,20},{6,21},{7,22},{9,24},{10,25},{11,26},{... | collective-permute-start | bytes 147464 | tf_op jit(solution)/shard_map/ppermute | solution.py:198
  54.1 0.0 collective-permute-done.10.refs_11_
  54.1 2.8 %collective-permute-start.15 = (bf16[3,64,128]{2,1,0:T(8,128)(2,1)S(1)}, bf16[3,64,128]{2,1,0:T(8,128)(2,1)S(1)}, u32[]{:S(2)}, u32[]{:S(2)}) collective-permute-start(bf16[3,64,128]{2,1,0:T(8,128)(2,1)S(1)} %get-tuple-element.53), channel_id=1, source_target_pairs={{0,16},{1,17},{2,18},{4,20},{5,21},{6,22},{8,24},{9,25},{10,26},{1... | collective-permute-start | bytes 147464 | tf_op jit(solution)/shard_map/ppermute | solution.py:198
  57.0 0.0 collective-permute-done.11.refs_12_
  57.0 1.3 collective-permute-start.16
  58.3 0.0 collective-permute-done.12.refs_13_
  58.3 6.7 %collective-permute-start.17 = (bf16[3,64,128]{2,1,0:T(8,128)(2,1)S(1)}, bf16[3,64,128]{2,1,0:T(8,128)(2,1)S(1)}, u32[]{:S(2)}, u32[]{:S(2)}) collective-permute-start(bf16[3,64,128]{2,1,0:T(8,128)(2,1)S(1)} %get-tuple-element.55), channel_id=1, source_target_pairs={{0,18},{2,20},{3,21},{4,22},{6,24},{7,25},{8,26},{10,28},{11,29},{... | collective-permute-start | bytes 147464 | tf_op jit(solution)/shard_map/ppermute | solution.py:198
  65.0 1.9 %collective-permute-start.18 = (bf16[3,64,128]{2,1,0:T(8,128)(2,1)S(1)}, bf16[3,64,128]{2,1,0:T(8,128)(2,1)S(1)}, u32[]{:S(2)}, u32[]{:S(2)}) collective-permute-start(bf16[3,64,128]{2,1,0:T(8,128)(2,1)S(1)} %get-tuple-element.56), channel_id=1, source_target_pairs={{1,20},{2,21},{3,22},{5,24},{6,25},{7,26},{9,28},{10,29},{11,30},{... | collective-permute-start | bytes 147464 | tf_op jit(solution)/shard_map/ppermute | solution.py:198
  67.0 0.0 collective-permute-done.14.refs_15_
  67.0 3.8 %collective-permute-start.19 = (bf16[3,64,128]{2,1,0:T(8,128)(2,1)S(1)}, bf16[3,64,128]{2,1,0:T(8,128)(2,1)S(1)}, u32[]{:S(2)}, u32[]{:S(2)}) collective-permute-start(bf16[3,64,128]{2,1,0:T(8,128)(2,1)S(1)} %get-tuple-element.57), channel_id=1, source_target_pairs={{0,20},{1,21},{2,22},{4,24},{5,25},{6,26},{8,28},{9,29},{10,30},{1... | collective-permute-start | bytes 147464 | tf_op jit(solution)/shard_map/ppermute | solution.py:198
  70.8 0.0 collective-permute-done.15.refs_16_
  70.8 1.3 collective-permute-start.20
  72.1 6.8 %collective-permute-start.21 = (bf16[3,64,128]{2,1,0:T(8,128)(2,1)S(1)}, bf16[3,64,128]{2,1,0:T(8,128)(2,1)S(1)}, u32[]{:S(2)}, u32[]{:S(2)}) collective-permute-start(bf16[3,64,128]{2,1,0:T(8,128)(2,1)S(1)} %get-tuple-element.59), channel_id=1, source_target_pairs={{0,22},{2,24},{3,25},{4,26},{6,28},{7,29},{8,30},{10,0},{11,1},{12... | collective-permute-start | bytes 147464 | tf_op jit(solution)/shard_map/ppermute | solution.py:198
  78.9 0.0 collective-permute-done.17.refs_18_
  78.9 1.9 %collective-permute-start.22 = (bf16[3,64,128]{2,1,0:T(8,128)(2,1)S(1)}, bf16[3,64,128]{2,1,0:T(8,128)(2,1)S(1)}, u32[]{:S(2)}, u32[]{:S(2)}) collective-permute-start(bf16[3,64,128]{2,1,0:T(8,128)(2,1)S(1)} %get-tuple-element.60), channel_id=1, source_target_pairs={{1,24},{2,25},{3,26},{5,28},{6,29},{7,30},{9,0},{10,1},{11,2},{13,... | collective-permute-start | bytes 147464 | tf_op jit(solution)/shard_map/ppermute | solution.py:198
  80.9 3.6 %collective-permute-start.23 = (bf16[3,64,128]{2,1,0:T(8,128)(2,1)S(1)}, bf16[3,64,128]{2,1,0:T(8,128)(2,1)S(1)}, u32[]{:S(2)}, u32[]{:S(2)}) collective-permute-start(bf16[3,64,128]{2,1,0:T(8,128)(2,1)S(1)} %get-tuple-element.61), channel_id=1, source_target_pairs={{0,24},{1,25},{2,26},{4,28},{5,29},{6,30},{8,0},{9,1},{10,2},{12,4... | collective-permute-start | bytes 147464 | tf_op jit(solution)/shard_map/ppermute | solution.py:198
  84.4 1.3 collective-permute-start.24
  85.7 0.0 collective-permute-done.20.refs_21_
  85.7 6.4 %collective-permute-start.25 = (bf16[3,64,128]{2,1,0:T(8,128)(2,1)S(1)}, bf16[3,64,128]{2,1,0:T(8,128)(2,1)S(1)}, u32[]{:S(2)}, u32[]{:S(2)}) collective-permute-start(bf16[3,64,128]{2,1,0:T(8,128)(2,1)S(1)} %get-tuple-element.63), channel_id=1, source_target_pairs={{0,26},{2,28},{3,29},{4,30},{6,0},{7,1},{8,2},{10,4},{11,5},{12,6}... | collective-permute-start | bytes 147464 | tf_op jit(solution)/shard_map/ppermute | solution.py:198
  92.1 0.0 collective-permute-done.21.refs_22_
  92.1 1.9 %collective-permute-start.26 = (bf16[3,64,128]{2,1,0:T(8,128)(2,1)S(1)}, bf16[3,64,128]{2,1,0:T(8,128)(2,1)S(1)}, u32[]{:S(2)}, u32[]{:S(2)}) collective-permute-start(bf16[3,64,128]{2,1,0:T(8,128)(2,1)S(1)} %get-tuple-element.64), channel_id=1, source_target_pairs={{1,28},{2,29},{3,30},{5,0},{6,1},{7,2},{9,4},{10,5},{11,6},{13,8},... | collective-permute-start | bytes 147464 | tf_op jit(solution)/shard_map/ppermute | solution.py:198
  94.1 0.0 collective-permute-done.22.refs_23_
  94.1 3.0 %collective-permute-start.27 = (bf16[3,64,128]{2,1,0:T(8,128)(2,1)S(1)}, bf16[3,64,128]{2,1,0:T(8,128)(2,1)S(1)}, u32[]{:S(2)}, u32[]{:S(2)}) collective-permute-start(bf16[3,64,128]{2,1,0:T(8,128)(2,1)S(1)} %get-tuple-element.65), channel_id=1, source_target_pairs={{0,28},{1,29},{2,30},{4,0},{5,1},{6,2},{8,4},{9,5},{10,6},{12,8},{... | collective-permute-start | bytes 147464 | tf_op jit(solution)/shard_map/ppermute | solution.py:198
  97.1 0.0 collective-permute-done.23.refs_24_
  97.1 1.3 collective-permute-start.28
  98.4 0.0 copy-start.4
  98.4 5.5 %collective-permute-start.29 = (bf16[3,64,128]{2,1,0:T(8,128)(2,1)S(1)}, bf16[3,64,128]{2,1,0:T(8,128)(2,1)S(1)}, u32[]{:S(2)}, u32[]{:S(2)}) collective-permute-start(bf16[3,64,128]{2,1,0:T(8,128)(2,1)S(1)} %get-tuple-element.67), channel_id=1, source_target_pairs={{0,30},{2,0},{3,1},{4,2},{6,4},{7,5},{8,6},{10,8},{11,9},{12,10},{... | collective-permute-start | bytes 147464 | tf_op jit(solution)/shard_map/ppermute | solution.py:198
  103.9 0.0 collective-permute-done.25.refs_26_
  103.9 0.0 copy-start.5
  104.0 0.0 copy-start.6
  104.0 1.9 %collective-permute-start.30 = (bf16[3,64,128]{2,1,0:T(8,128)(2,1)S(1)}, bf16[3,64,128]{2,1,0:T(8,128)(2,1)S(1)}, u32[]{:S(2)}, u32[]{:S(2)}) collective-permute-start(bf16[3,64,128]{2,1,0:T(8,128)(2,1)S(1)} %get-tuple-element.68), channel_id=1, source_target_pairs={{1,0},{2,1},{3,2},{5,4},{6,5},{7,6},{9,8},{10,9},{11,10},{13,12},{... | collective-permute-start | bytes 147464 | tf_op jit(solution)/shard_map/ppermute | solution.py:198
  105.9 0.0 collective-permute-done.26.refs_27_
  105.9 0.0 collective-permute-done.27.refs_28_
  105.9 0.0 collective-permute-done.29.refs_30_
  105.9 3.3 %collective-permute-done.30.refs_31_ = bf16[3,64,128]{2,1,0:T(8,128)(2,1)S(1)} collective-permute-done((bf16[3,64,128]{2,1,0:T(8,128)(2,1)S(1)}, bf16[3,64,128]{2,1,0:T(8,128)(2,1)S(1)}, u32[]{:S(2)}, u32[]{:S(2)}) %collective-permute-start.30) | collective-permute-done | bytes 49184 | tf_op jit(solution)/shard_map/ppermute | solution.py:198
  109.2 7.4 %attention.1 = bf16[32,64,128]{2,1,0:T(8,128)(2,1)S(1)} custom-call(s32[4]{0:T(128)S(1)} %copy-done.5, s32[4]{0:T(128)S(1)} %copy-done.6, s32[4,4]{1,0:T(4,128)S(1)} %copy-done.4, s32[3]{0:T(128)S(1)} %pad_add_fusion.place_ref, f32[8,3072]{1,0:T(8,128)S(1)} %copy-done.3, bf16[3,64,128]{2,1,0:T(8,128)(2,1)S(1)} %get-tuple-element.37.refs_0_, ...), custom_call_target="tpu_custom_call" | custom-call | tf_op jit(solution)/shard_map/attention/pallas_call | solution.py:199
  116.7 18.1 %all_to_all.5.in_ref = bf16[32,64,128]{2,1,0:T(8,128)(2,1)S(1)} all-to-all(bf16[32,64,128]{2,1,0:T(8,128)(2,1)S(1)} %attention.1), channel_id=1, replica_groups=mesh['seq'=16,'head'=2] {'seq','head'}, dimensions={0} | all-to-all | bytes 1048576 | tf_op jit(solution)/shard_map/all_to_all | solution.py:208
  134.7 0.8 unpack.1
  (17 shorter events, 0.0 us)
Async XLA Ops:
  0.1 1.0 copy-start
  1.1 1.0 copy-start.1
  2.1 1.0 copy-start.2
  3.1 106.2 %copy-start.3 = (f32[8,3072]{1,0:T(8,128)S(1)}, f32[8,3072]{1,0:T(8,128)}, u32[]{:S(2)}) copy-start(f32[8,3072]{1,0:T(8,128)} %gate_ref.1) | copy-start | bytes 294916
  4.1 14.3 %collective-permute-start = (bf16[3,64,128]{2,1,0:T(8,128)(2,1)S(1)}, bf16[3,64,128]{2,1,0:T(8,128)(2,1)S(1)}, u32[]{:S(2)}, u32[]{:S(2)}) collective-permute-start(bf16[3,64,128]{2,1,0:T(8,128)(2,1)S(1)} %get-tuple-element.38), channel_id=1, source_target_pairs={{0,1},{1,2},{3,4},{4,5},{5,6},{7,8},{8,9},{9,10},{11,12},{12,13},{... | collective-permute-start | bytes 147464 | tf_op jit(solution)/shard_map/ppermute | solution.py:198
  5.4 19.9 %collective-permute-start.1 = (bf16[3,64,128]{2,1,0:T(8,128)(2,1)S(1)}, bf16[3,64,128]{2,1,0:T(8,128)(2,1)S(1)}, u32[]{:S(2)}, u32[]{:S(2)}) collective-permute-start(bf16[3,64,128]{2,1,0:T(8,128)(2,1)S(1)} %get-tuple-element.39), channel_id=1, source_target_pairs={{0,2},{2,4},{3,5},{4,6},{6,8},{7,9},{8,10},{10,12},{11,13},{12,14}... | collective-permute-start | bytes 147464 | tf_op jit(solution)/shard_map/ppermute | solution.py:198
  12.0 15.1 %collective-permute-start.2 = (bf16[3,64,128]{2,1,0:T(8,128)(2,1)S(1)}, bf16[3,64,128]{2,1,0:T(8,128)(2,1)S(1)}, u32[]{:S(2)}, u32[]{:S(2)}) collective-permute-start(bf16[3,64,128]{2,1,0:T(8,128)(2,1)S(1)} %get-tuple-element.40), channel_id=1, source_target_pairs={{1,4},{2,5},{3,6},{5,8},{6,9},{7,10},{9,12},{10,13},{11,14},{13,16... | collective-permute-start | bytes 147464 | tf_op jit(solution)/shard_map/ppermute | solution.py:198
  13.9 16.4 %collective-permute-start.3 = (bf16[3,64,128]{2,1,0:T(8,128)(2,1)S(1)}, bf16[3,64,128]{2,1,0:T(8,128)(2,1)S(1)}, u32[]{:S(2)}, u32[]{:S(2)}) collective-permute-start(bf16[3,64,128]{2,1,0:T(8,128)(2,1)S(1)} %get-tuple-element.41), channel_id=1, source_target_pairs={{0,4},{1,5},{2,6},{4,8},{5,9},{6,10},{8,12},{9,13},{10,14},{12,16}... | collective-permute-start | bytes 147464 | tf_op jit(solution)/shard_map/ppermute | solution.py:198
  17.1 14.6 %collective-permute-start.4 = (bf16[3,64,128]{2,1,0:T(8,128)(2,1)S(1)}, bf16[3,64,128]{2,1,0:T(8,128)(2,1)S(1)}, u32[]{:S(2)}, u32[]{:S(2)}) collective-permute-start(bf16[3,64,128]{2,1,0:T(8,128)(2,1)S(1)} %get-tuple-element.42), channel_id=1, source_target_pairs={{0,5},{1,6},{3,8},{4,9},{5,10},{7,12},{8,13},{9,14},{11,16},{12,17... | collective-permute-start | bytes 147464 | tf_op jit(solution)/shard_map/ppermute | solution.py:198
  18.4 19.8 %collective-permute-start.5 = (bf16[3,64,128]{2,1,0:T(8,128)(2,1)S(1)}, bf16[3,64,128]{2,1,0:T(8,128)(2,1)S(1)}, u32[]{:S(2)}, u32[]{:S(2)}) collective-permute-start(bf16[3,64,128]{2,1,0:T(8,128)(2,1)S(1)} %get-tuple-element.43), channel_id=1, source_target_pairs={{0,6},{2,8},{3,9},{4,10},{6,12},{7,13},{8,14},{10,16},{11,17},{12,... | collective-permute-start | bytes 147464 | tf_op jit(solution)/shard_map/ppermute | solution.py:198
  25.2 14.9 %collective-permute-start.6 = (bf16[3,64,128]{2,1,0:T(8,128)(2,1)S(1)}, bf16[3,64,128]{2,1,0:T(8,128)(2,1)S(1)}, u32[]{:S(2)}, u32[]{:S(2)}) collective-permute-start(bf16[3,64,128]{2,1,0:T(8,128)(2,1)S(1)} %get-tuple-element.44), channel_id=1, source_target_pairs={{1,8},{2,9},{3,10},{5,12},{6,13},{7,14},{9,16},{10,17},{11,18},{13... | collective-permute-start | bytes 147464 | tf_op jit(solution)/shard_map/ppermute | solution.py:198
  27.2 17.1 %collective-permute-start.7 = (bf16[3,64,128]{2,1,0:T(8,128)(2,1)S(1)}, bf16[3,64,128]{2,1,0:T(8,128)(2,1)S(1)}, u32[]{:S(2)}, u32[]{:S(2)}) collective-permute-start(bf16[3,64,128]{2,1,0:T(8,128)(2,1)S(1)} %get-tuple-element.45), channel_id=1, source_target_pairs={{0,8},{1,9},{2,10},{4,12},{5,13},{6,14},{8,16},{9,17},{10,18},{12,... | collective-permute-start | bytes 147464 | tf_op jit(solution)/shard_map/ppermute | solution.py:198
  30.4 15.2 %collective-permute-start.8 = (bf16[3,64,128]{2,1,0:T(8,128)(2,1)S(1)}, bf16[3,64,128]{2,1,0:T(8,128)(2,1)S(1)}, u32[]{:S(2)}, u32[]{:S(2)}) collective-permute-start(bf16[3,64,128]{2,1,0:T(8,128)(2,1)S(1)} %get-tuple-element.46), channel_id=1, source_target_pairs={{0,9},{1,10},{3,12},{4,13},{5,14},{7,16},{8,17},{9,18},{11,20},{12... | collective-permute-start | bytes 147464 | tf_op jit(solution)/shard_map/ppermute | solution.py:198
  31.7 20.5 %collective-permute-start.9 = (bf16[3,64,128]{2,1,0:T(8,128)(2,1)S(1)}, bf16[3,64,128]{2,1,0:T(8,128)(2,1)S(1)}, u32[]{:S(2)}, u32[]{:S(2)}) collective-permute-start(bf16[3,64,128]{2,1,0:T(8,128)(2,1)S(1)} %get-tuple-element.47), channel_id=1, source_target_pairs={{0,10},{2,12},{3,13},{4,14},{6,16},{7,17},{8,18},{10,20},{11,21},{... | collective-permute-start | bytes 147464 | tf_op jit(solution)/shard_map/ppermute | solution.py:198
  38.2 16.0 %collective-permute-start.10 = (bf16[3,64,128]{2,1,0:T(8,128)(2,1)S(1)}, bf16[3,64,128]{2,1,0:T(8,128)(2,1)S(1)}, u32[]{:S(2)}, u32[]{:S(2)}) collective-permute-start(bf16[3,64,128]{2,1,0:T(8,128)(2,1)S(1)} %get-tuple-element.48), channel_id=1, source_target_pairs={{1,12},{2,13},{3,14},{5,16},{6,17},{7,18},{9,20},{10,21},{11,22},{... | collective-permute-start | bytes 147464 | tf_op jit(solution)/shard_map/ppermute | solution.py:198
  40.1 16.9 %collective-permute-start.11 = (bf16[3,64,128]{2,1,0:T(8,128)(2,1)S(1)}, bf16[3,64,128]{2,1,0:T(8,128)(2,1)S(1)}, u32[]{:S(2)}, u32[]{:S(2)}) collective-permute-start(bf16[3,64,128]{2,1,0:T(8,128)(2,1)S(1)} %get-tuple-element.49), channel_id=1, source_target_pairs={{0,12},{1,13},{2,14},{4,16},{5,17},{6,18},{8,20},{9,21},{10,22},{1... | collective-permute-start | bytes 147464 | tf_op jit(solution)/shard_map/ppermute | solution.py:198
  44.3 14.0 %collective-permute-start.12 = (bf16[3,64,128]{2,1,0:T(8,128)(2,1)S(1)}, bf16[3,64,128]{2,1,0:T(8,128)(2,1)S(1)}, u32[]{:S(2)}, u32[]{:S(2)}) collective-permute-start(bf16[3,64,128]{2,1,0:T(8,128)(2,1)S(1)} %get-tuple-element.50), channel_id=1, source_target_pairs={{0,13},{1,14},{3,16},{4,17},{5,18},{7,20},{8,21},{9,22},{11,24},{1... | collective-permute-start | bytes 147464 | tf_op jit(solution)/shard_map/ppermute | solution.py:198
  45.6 19.4 %collective-permute-start.13 = (bf16[3,64,128]{2,1,0:T(8,128)(2,1)S(1)}, bf16[3,64,128]{2,1,0:T(8,128)(2,1)S(1)}, u32[]{:S(2)}, u32[]{:S(2)}) collective-permute-start(bf16[3,64,128]{2,1,0:T(8,128)(2,1)S(1)} %get-tuple-element.51), channel_id=1, source_target_pairs={{0,14},{2,16},{3,17},{4,18},{6,20},{7,21},{8,22},{10,24},{11,25},{... | collective-permute-start | bytes 147464 | tf_op jit(solution)/shard_map/ppermute | solution.py:198
  52.2 14.7 %collective-permute-start.14 = (bf16[3,64,128]{2,1,0:T(8,128)(2,1)S(1)}, bf16[3,64,128]{2,1,0:T(8,128)(2,1)S(1)}, u32[]{:S(2)}, u32[]{:S(2)}) collective-permute-start(bf16[3,64,128]{2,1,0:T(8,128)(2,1)S(1)} %get-tuple-element.52), channel_id=1, source_target_pairs={{1,16},{2,17},{3,18},{5,20},{6,21},{7,22},{9,24},{10,25},{11,26},{... | collective-permute-start | bytes 147464 | tf_op jit(solution)/shard_map/ppermute | solution.py:198
  54.1 16.6 %collective-permute-start.15 = (bf16[3,64,128]{2,1,0:T(8,128)(2,1)S(1)}, bf16[3,64,128]{2,1,0:T(8,128)(2,1)S(1)}, u32[]{:S(2)}, u32[]{:S(2)}) collective-permute-start(bf16[3,64,128]{2,1,0:T(8,128)(2,1)S(1)} %get-tuple-element.53), channel_id=1, source_target_pairs={{0,16},{1,17},{2,18},{4,20},{5,21},{6,22},{8,24},{9,25},{10,26},{1... | collective-permute-start | bytes 147464 | tf_op jit(solution)/shard_map/ppermute | solution.py:198
  57.0 15.1 %collective-permute-start.16 = (bf16[3,64,128]{2,1,0:T(8,128)(2,1)S(1)}, bf16[3,64,128]{2,1,0:T(8,128)(2,1)S(1)}, u32[]{:S(2)}, u32[]{:S(2)}) collective-permute-start(bf16[3,64,128]{2,1,0:T(8,128)(2,1)S(1)} %get-tuple-element.54), channel_id=1, source_target_pairs={{0,17},{1,18},{3,20},{4,21},{5,22},{7,24},{8,25},{9,26},{11,28},{1... | collective-permute-start | bytes 147464 | tf_op jit(solution)/shard_map/ppermute | solution.py:198
  58.3 20.6 %collective-permute-start.17 = (bf16[3,64,128]{2,1,0:T(8,128)(2,1)S(1)}, bf16[3,64,128]{2,1,0:T(8,128)(2,1)S(1)}, u32[]{:S(2)}, u32[]{:S(2)}) collective-permute-start(bf16[3,64,128]{2,1,0:T(8,128)(2,1)S(1)} %get-tuple-element.55), channel_id=1, source_target_pairs={{0,18},{2,20},{3,21},{4,22},{6,24},{7,25},{8,26},{10,28},{11,29},{... | collective-permute-start | bytes 147464 | tf_op jit(solution)/shard_map/ppermute | solution.py:198
  65.0 15.8 %collective-permute-start.18 = (bf16[3,64,128]{2,1,0:T(8,128)(2,1)S(1)}, bf16[3,64,128]{2,1,0:T(8,128)(2,1)S(1)}, u32[]{:S(2)}, u32[]{:S(2)}) collective-permute-start(bf16[3,64,128]{2,1,0:T(8,128)(2,1)S(1)} %get-tuple-element.56), channel_id=1, source_target_pairs={{1,20},{2,21},{3,22},{5,24},{6,25},{7,26},{9,28},{10,29},{11,30},{... | collective-permute-start | bytes 147464 | tf_op jit(solution)/shard_map/ppermute | solution.py:198
  67.0 17.5 %collective-permute-start.19 = (bf16[3,64,128]{2,1,0:T(8,128)(2,1)S(1)}, bf16[3,64,128]{2,1,0:T(8,128)(2,1)S(1)}, u32[]{:S(2)}, u32[]{:S(2)}) collective-permute-start(bf16[3,64,128]{2,1,0:T(8,128)(2,1)S(1)} %get-tuple-element.57), channel_id=1, source_target_pairs={{0,20},{1,21},{2,22},{4,24},{5,25},{6,26},{8,28},{9,29},{10,30},{1... | collective-permute-start | bytes 147464 | tf_op jit(solution)/shard_map/ppermute | solution.py:198
  70.8 14.9 %collective-permute-start.20 = (bf16[3,64,128]{2,1,0:T(8,128)(2,1)S(1)}, bf16[3,64,128]{2,1,0:T(8,128)(2,1)S(1)}, u32[]{:S(2)}, u32[]{:S(2)}) collective-permute-start(bf16[3,64,128]{2,1,0:T(8,128)(2,1)S(1)} %get-tuple-element.58), channel_id=1, source_target_pairs={{0,21},{1,22},{3,24},{4,25},{5,26},{7,28},{8,29},{9,30},{11,0},{12... | collective-permute-start | bytes 147464 | tf_op jit(solution)/shard_map/ppermute | solution.py:198
  72.1 20.0 %collective-permute-start.21 = (bf16[3,64,128]{2,1,0:T(8,128)(2,1)S(1)}, bf16[3,64,128]{2,1,0:T(8,128)(2,1)S(1)}, u32[]{:S(2)}, u32[]{:S(2)}) collective-permute-start(bf16[3,64,128]{2,1,0:T(8,128)(2,1)S(1)} %get-tuple-element.59), channel_id=1, source_target_pairs={{0,22},{2,24},{3,25},{4,26},{6,28},{7,29},{8,30},{10,0},{11,1},{12... | collective-permute-start | bytes 147464 | tf_op jit(solution)/shard_map/ppermute | solution.py:198
  78.9 15.1 %collective-permute-start.22 = (bf16[3,64,128]{2,1,0:T(8,128)(2,1)S(1)}, bf16[3,64,128]{2,1,0:T(8,128)(2,1)S(1)}, u32[]{:S(2)}, u32[]{:S(2)}) collective-permute-start(bf16[3,64,128]{2,1,0:T(8,128)(2,1)S(1)} %get-tuple-element.60), channel_id=1, source_target_pairs={{1,24},{2,25},{3,26},{5,28},{6,29},{7,30},{9,0},{10,1},{11,2},{13,... | collective-permute-start | bytes 147464 | tf_op jit(solution)/shard_map/ppermute | solution.py:198
  80.9 16.2 %collective-permute-start.23 = (bf16[3,64,128]{2,1,0:T(8,128)(2,1)S(1)}, bf16[3,64,128]{2,1,0:T(8,128)(2,1)S(1)}, u32[]{:S(2)}, u32[]{:S(2)}) collective-permute-start(bf16[3,64,128]{2,1,0:T(8,128)(2,1)S(1)} %get-tuple-element.61), channel_id=1, source_target_pairs={{0,24},{1,25},{2,26},{4,28},{5,29},{6,30},{8,0},{9,1},{10,2},{12,4... | collective-permute-start | bytes 147464 | tf_op jit(solution)/shard_map/ppermute | solution.py:198
  84.4 14.0 %collective-permute-start.24 = (bf16[3,64,128]{2,1,0:T(8,128)(2,1)S(1)}, bf16[3,64,128]{2,1,0:T(8,128)(2,1)S(1)}, u32[]{:S(2)}, u32[]{:S(2)}) collective-permute-start(bf16[3,64,128]{2,1,0:T(8,128)(2,1)S(1)} %get-tuple-element.62), channel_id=1, source_target_pairs={{0,25},{1,26},{3,28},{4,29},{5,30},{7,0},{8,1},{9,2},{11,4},{12,5}... | collective-permute-start | bytes 147464 | tf_op jit(solution)/shard_map/ppermute | solution.py:198
  85.7 18.2 %collective-permute-start.25 = (bf16[3,64,128]{2,1,0:T(8,128)(2,1)S(1)}, bf16[3,64,128]{2,1,0:T(8,128)(2,1)S(1)}, u32[]{:S(2)}, u32[]{:S(2)}) collective-permute-start(bf16[3,64,128]{2,1,0:T(8,128)(2,1)S(1)} %get-tuple-element.63), channel_id=1, source_target_pairs={{0,26},{2,28},{3,29},{4,30},{6,0},{7,1},{8,2},{10,4},{11,5},{12,6}... | collective-permute-start | bytes 147464 | tf_op jit(solution)/shard_map/ppermute | solution.py:198
  92.1 13.8 %collective-permute-start.26 = (bf16[3,64,128]{2,1,0:T(8,128)(2,1)S(1)}, bf16[3,64,128]{2,1,0:T(8,128)(2,1)S(1)}, u32[]{:S(2)}, u32[]{:S(2)}) collective-permute-start(bf16[3,64,128]{2,1,0:T(8,128)(2,1)S(1)} %get-tuple-element.64), channel_id=1, source_target_pairs={{1,28},{2,29},{3,30},{5,0},{6,1},{7,2},{9,4},{10,5},{11,6},{13,8},... | collective-permute-start | bytes 147464 | tf_op jit(solution)/shard_map/ppermute | solution.py:198
  94.1 11.8 %collective-permute-start.27 = (bf16[3,64,128]{2,1,0:T(8,128)(2,1)S(1)}, bf16[3,64,128]{2,1,0:T(8,128)(2,1)S(1)}, u32[]{:S(2)}, u32[]{:S(2)}) collective-permute-start(bf16[3,64,128]{2,1,0:T(8,128)(2,1)S(1)} %get-tuple-element.65), channel_id=1, source_target_pairs={{0,28},{1,29},{2,30},{4,0},{5,1},{6,2},{8,4},{9,5},{10,6},{12,8},{... | collective-permute-start | bytes 147464 | tf_op jit(solution)/shard_map/ppermute | solution.py:198
  97.1 8.8 %collective-permute-start.28 = (bf16[3,64,128]{2,1,0:T(8,128)(2,1)S(1)}, bf16[3,64,128]{2,1,0:T(8,128)(2,1)S(1)}, u32[]{:S(2)}, u32[]{:S(2)}) collective-permute-start(bf16[3,64,128]{2,1,0:T(8,128)(2,1)S(1)} %get-tuple-element.66), channel_id=1, source_target_pairs={{0,29},{1,30},{3,0},{4,1},{5,2},{7,4},{8,5},{9,6},{11,8},{12,9},{1... | collective-permute-start | bytes 147464 | tf_op jit(solution)/shard_map/ppermute | solution.py:198
  98.4 10.8 %copy-start.4 = (s32[4,4]{1,0:T(4,128)S(1)}, s32[4,4]{1,0:T(4,128)}, u32[]{:S(2)}) copy-start(s32[4,4]{1,0:T(4,128)} %mask_ref.1) | copy-start | bytes 196
  98.4 7.5 %collective-permute-start.29 = (bf16[3,64,128]{2,1,0:T(8,128)(2,1)S(1)}, bf16[3,64,128]{2,1,0:T(8,128)(2,1)S(1)}, u32[]{:S(2)}, u32[]{:S(2)}) collective-permute-start(bf16[3,64,128]{2,1,0:T(8,128)(2,1)S(1)} %get-tuple-element.67), channel_id=1, source_target_pairs={{0,30},{2,0},{3,1},{4,2},{6,4},{7,5},{8,6},{10,8},{11,9},{12,10},{... | collective-permute-start | bytes 147464 | tf_op jit(solution)/shard_map/ppermute | solution.py:198
  103.9 5.3 %copy-start.5 = (s32[4]{0:T(128)S(1)}, s32[4]{0:T(128)}, u32[]{:S(2)}) copy-start(s32[4]{0:T(128)} %counts_ref.1) | copy-start | bytes 52
  104.0 5.3 %copy-start.6 = (s32[4]{0:T(128)S(1)}, s32[4]{0:T(128)}, u32[]{:S(2)}) copy-start(s32[4]{0:T(128)} %plan_ref.1) | copy-start | bytes 52
  104.0 5.3 %collective-permute-start.30 = (bf16[3,64,128]{2,1,0:T(8,128)(2,1)S(1)}, bf16[3,64,128]{2,1,0:T(8,128)(2,1)S(1)}, u32[]{:S(2)}, u32[]{:S(2)}) collective-permute-start(bf16[3,64,128]{2,1,0:T(8,128)(2,1)S(1)} %get-tuple-element.68), channel_id=1, source_target_pairs={{1,0},{2,1},{3,2},{5,4},{6,5},{7,6},{9,8},{10,9},{11,10},{13,12},{... | collective-permute-start | bytes 147464 | tf_op jit(solution)/shard_map/ppermute | solution.py:198

commit v4 on v2

--- a/solution.py
+++ b/solution.py
@@ -97,16 +97,37 @@
     return lax.all_to_all(result, "head", split_axis=0, concat_axis=1, tiled=True)
 
 
-def pack_kernel(parts, held, q_ref, k_ref, v_ref, out_ref):
+def pack_kernel(parts, held, *refs):
+    count = (len(refs) - 2) // 2
+    in_refs, out_ref, bufs, sems = refs[:count], refs[count], refs[count + 1 : -1], refs[-1]
     slots = out_ref.shape[0] // parts
-    for p in range(parts):
-        for s in range(slots):
-            for i, ref in enumerate((q_ref, k_ref, v_ref)):
-                if s < held:
-                    h = p * held + s
-                    out_ref[p * slots + s, i] = ref[:, h * HEAD_DIM : (h + 1) * HEAD_DIM]
-                else:
-                    out_ref[p * slots + s, i] = jnp.zeros(out_ref.shape[2:], out_ref.dtype)
+    copies = [pltpu.make_async_copy(in_refs[i], bufs[i], sems.at[i]) for i in range(count)]
+    for copy in copies:
+        copy.start()
+    for s in range(held, slots):
+        for p in range(parts):
+            out_ref[p * slots + s] = jnp.zeros(out_ref.shape[1:], out_ref.dtype)
+    for i, copy in enumerate(copies):
+        copy.wait()
+        for p in range(parts):
+            for s in range(held):
+                h = p * held + s
+                out_ref[p * slots + s, i] = bufs[i][:, h * HEAD_DIM : (h + 1) * HEAD_DIM]
+
+
+def pack(arrays, parts, held, n_dev):
+    local, feat = arrays[0].shape
+    count = len(arrays)
+    return pl.pallas_call(
+        functools.partial(pack_kernel, parts, held),
+        out_shape=jax.ShapeDtypeStruct((n_dev, count, local, HEAD_DIM), jnp.bfloat16),
+        in_specs=[pl.BlockSpec(memory_space=pl.ANY)] * count,
+        out_specs=pl.BlockSpec(memory_space=pltpu.VMEM),
+        scratch_shapes=[pltpu.VMEM((local, feat), jnp.bfloat16)] * count + [pltpu.SemaphoreType.DMA((count,))],
+        compiler_params=pltpu.CompilerParams(vmem_limit_bytes=60 * 1024 * 1024),
+        cost_estimate=pl.CostEstimate(flops=0, bytes_accessed=count * local * feat * 5, transcendentals=0),
+        name="pack",
+    )(*arrays)
 
 
 def unpack_kernel(parts, held, in_ref, out_ref):
@@ -117,25 +138,20 @@
             out_ref[:, h * HEAD_DIM : (h + 1) * HEAD_DIM] = in_ref[p * slots + s]
 
 
-def attention_kernel(block, counts_ref, plan_ref, mask_ref, place_ref, got_ref, gate_ref, out_ref):
+def weights_kernel(block, counts_ref, mask_ref, place_ref, got_ref, weights_ref, total_ref):
     n_dev, _, local, _ = got_ref.shape
     per_group = n_dev // GROUPS
     group_tok = per_group * local
     rows = block * local
     factor = math.log2(math.e) / math.sqrt(HEAD_DIM)
-    head = place_ref[0]
-    busy = place_ref[1]
-
-    @pl.when(busy == 1)
+
+    @pl.when(place_ref[1] == 1)
     def _():
-        gates = gate_ref[:, pl.ds(pl.multiple_of(head * HEAD_DIM, HEAD_DIM), HEAD_DIM)]
-        level = lax.broadcasted_iota(jnp.int32, (LEVELS, HEAD_DIM), 0)
         for c in range(GROUPS):
             width = (c + 1) * group_tok
             column = lax.broadcasted_iota(jnp.int32, (1, group_tok), 1)
             limits = [counts_ref[d] * mask_ref[c, d] for d in range(c + 1)]
             allowed = jnp.concatenate([column < limits[d] for d in range(c + 1)], axis=1)
-            gate = jnp.sum(jnp.where(level == plan_ref[c], gates, jnp.float32(0.0)), axis=0, keepdims=True)
 
             @pl.loop(0, per_group // block)
             def _(step):
@@ -149,15 +165,41 @@
                 scores = jnp.where(allowed, scores, jnp.float32(-1e30))
                 top = jnp.max(scores, axis=1, keepdims=True)
                 weights = jnp.exp2(scores * factor - top * factor)
+                row = pl.multiple_of(step * rows, rows)
                 total = jnp.sum(weights, axis=1, keepdims=True)
-                mixed = jnp.dot(
-                    weights.astype(jnp.bfloat16),
-                    got_ref[: (c + 1) * per_group, 2].reshape(width, HEAD_DIM),
+                total_ref[c, pl.ds(row, rows), :] = jnp.broadcast_to(total, (rows, HEAD_DIM))
+                weights = weights.astype(jnp.bfloat16)
+                for d in range(c + 1):
+                    weights_ref[c * (c + 1) // 2 + d, pl.ds(row, rows), :] = weights[
+                        :, d * group_tok : (d + 1) * group_tok
+                    ]
+
+
+def mix_kernel(counts_ref, plan_ref, place_ref, weights_ref, total_ref, v_ref, gate_ref, out_ref):
+    n_dev, _, local, _ = v_ref.shape
+    per_group = n_dev // GROUPS
+    group_tok = per_group * local
+    head = place_ref[0]
+    busy = place_ref[1]
+
+    @pl.when(busy == 1)
+    def _():
+        gates = gate_ref[:, pl.ds(pl.multiple_of(head * HEAD_DIM, HEAD_DIM), HEAD_DIM)]
+        level = lax.broadcasted_iota(jnp.int32, (LEVELS, HEAD_DIM), 0)
+        for c in range(GROUPS):
+            gate = jnp.sum(jnp.where(level == plan_ref[c], gates, jnp.float32(0.0)), axis=0, keepdims=True)
+            mixed = jnp.zeros((group_tok, HEAD_DIM), jnp.float32)
+            for d in range(c + 1):
+                mixed += jnp.dot(
+                    weights_ref[c * (c + 1) // 2 + d],
+                    v_ref[d * per_group : (d + 1) * per_group, 0].reshape(group_tok, HEAD_DIM),
                     preferred_element_type=jnp.float32,
                 )
-                position = step * rows + lax.broadcasted_iota(jnp.int32, (rows, 1), 0)
-                mixed = jnp.where(position < counts_ref[c], mixed / total * gate, jnp.float32(0.0))
-                out_ref[pl.ds(first, block)] = mixed.astype(jnp.bfloat16).reshape(block, local, HEAD_DIM)
+            position = lax.broadcasted_iota(jnp.int32, (group_tok, 1), 0)
+            mixed = jnp.where(position < counts_ref[c], mixed / total_ref[c] * gate, jnp.float32(0.0))
+            out_ref[c * per_group : (c + 1) * per_group] = mixed.astype(jnp.bfloat16).reshape(
+                per_group, local, HEAD_DIM
+            )
 
     @pl.when(busy == 0)
     def _():
@@ -179,23 +221,32 @@
     smem = pl.BlockSpec(memory_space=pltpu.SMEM)
     vmem = pl.BlockSpec(memory_space=pltpu.VMEM)
 
-    sent = pl.pallas_call(
-        functools.partial(pack_kernel, parts, held),
-        out_shape=jax.ShapeDtypeStruct((n_dev, 3, local, HEAD_DIM), jnp.bfloat16),
-        in_specs=[vmem] * 3,
+    got = lax.all_to_all(pack((queries, keys), parts, held, n_dev), axes, split_axis=0, concat_axis=0, tiled=True)
+    got_v = lax.all_to_all(pack((values,), parts, held, n_dev), axes, split_axis=0, concat_axis=0, tiled=True)
+    group_tok = n_dev * local // GROUPS
+    pairs = GROUPS * (GROUPS + 1) // 2
+    work = pairs * group_tok * group_tok
+    weights, total = pl.pallas_call(
+        functools.partial(weights_kernel, max(1, 256 // local)),
+        out_shape=[
+            jax.ShapeDtypeStruct((pairs, group_tok, group_tok), jnp.bfloat16),
+            jax.ShapeDtypeStruct((GROUPS, group_tok, HEAD_DIM), jnp.float32),
+        ],
+        in_specs=[smem, smem, smem, vmem],
+        out_specs=[vmem, vmem],
+        compiler_params=pltpu.CompilerParams(vmem_limit_bytes=32 * 1024 * 1024),
+        cost_estimate=pl.CostEstimate(flops=2 * work * HEAD_DIM, bytes_accessed=work * 4, transcendentals=work),
+        name="weights",
+    )(counts, group_mask, place, got)
+    result = pl.pallas_call(
+        mix_kernel,
+        out_shape=jax.ShapeDtypeStruct((n_dev, local, HEAD_DIM), jnp.bfloat16),
+        in_specs=[smem, smem, smem, vmem, vmem, vmem, vmem],
         out_specs=vmem,
-        compiler_params=pltpu.CompilerParams(vmem_limit_bytes=16 * 1024 * 1024),
-        name="pack",
-    )(queries, keys, values)
-    got = lax.all_to_all(sent, axes, split_axis=0, concat_axis=0, tiled=True)
-    result = pl.pallas_call(
-        functools.partial(attention_kernel, max(1, 256 // local)),
-        out_shape=jax.ShapeDtypeStruct((n_dev, local, HEAD_DIM), jnp.bfloat16),
-        in_specs=[smem, smem, smem, smem, vmem, vmem],
-        out_specs=vmem,
-        compiler_params=pltpu.CompilerParams(vmem_limit_bytes=40 * 1024 * 1024),
-        name="attention",
-    )(counts, plan, group_mask, place, got, gate_table)
+        compiler_params=pltpu.CompilerParams(vmem_limit_bytes=32 * 1024 * 1024),
+        cost_estimate=pl.CostEstimate(flops=2 * work * HEAD_DIM, bytes_accessed=work * 2, transcendentals=0),
+        name="mix",
+    )(counts, plan, place, weights, total, got_v, gate_table)
     back = lax.all_to_all(result, axes, split_axis=0, concat_axis=0, tiled=True)
     return pl.pallas_call(
         functools.partial(unpack_kernel, parts, held),

time: 76.5 us -> 79.3 us (1.037)
  waiting for transfers between devices: 36.8 us -> 31.9 us
  starting transfers between devices: 7.1 us -> 11 us
  Pallas kernels: 9.28 us -> 12.6 us
  local copies, waits for them, and re-layouts: 3 us -> 4.8 us
  blocking collectives: 19.9 us -> 18.4 us
    all_to_all x1 -> x2, waiting for transfers between devices: 36.8 us -> 31.9 us  [the longest x1 24.1 us: head_each(): lax.all_to_all(pack((queries, keys), parts, held, n_dev), axes, split_axi...]
    all_to_all x1 -> x2, starting transfers between devices: 7.1 us -> 11 us  [the longest x1 7.1 us: head_each(): lax.all_to_all(pack((queries, keys), parts, held, n_dev), axes, split_axi...]
    pallas_call x2 -> x4, Pallas kernels: 8.46 us -> 11.8 us  [the longest x1 5.59 us: head_each(): pl.pallas_call(functools.partial(weights_kernel, max(1, 256 // local)), o...]
    unnamed x14 -> x12, local copies, waits for them, and re-layouts: 3 us -> 4.8 us
    all_to_all x1, blocking collectives: 19.9 us -> 18.4 us  [head_each(): back = lax.all_to_all(result, axes, split_axis=0, concat_axis=0, tiled=True)]
  transfers between devices with their start and end apart: 1 -> 2, of which waited for: 1 -> 2; matrix products, arithmetic and copies ran while one was open for 0% -> 0% of each run, Pallas kernels for 0% -> 10%
where the time goes in v4:
time: 79.3 us; the launch traced here: 78.9 us
  waiting for transfers between devices  31.9 us (40%)
  blocking collectives  18.4 us (23%)
  Pallas kernels  12.6 us (16%)
  starting transfers between devices  11 us (14%)
  local copies, waits for them, and re-layouts  4.8 us (6%)
    all_to_all x1, waiting for transfers between devices, head_each(): lax.all_to_all(pack((queries, keys), parts, held, n_dev), axes, split_axi...  24.1 us
    all_to_all x1, blocking collectives, head_each(): back = lax.all_to_all(result, axes, split_axis=0, concat_axis=0, tiled=True)  18.4 us
    all_to_all x1, waiting for transfers between devices, head_each(): lax.all_to_all(pack((values,), parts, held, n_dev), axes, split_axis=0, c...  7.82 us
    all_to_all x1, starting transfers between devices, head_each(): lax.all_to_all(pack((queries, keys), parts, held, n_dev), axes, split_axi...  7.1 us
    pallas_call x1, Pallas kernels, head_each(): pl.pallas_call(functools.partial(weights_kernel, max(1, 256 // local)), o...  5.59 us
    unnamed x12, local copies, waits for them, and re-layouts  4.8 us
    pallas_call x2, Pallas kernels, pack(): pl.pallas_call(functools.partial(pack_kernel, parts, held), out_shape=jax...  4.14 us
    all_to_all x1, starting transfers between devices, head_each(): lax.all_to_all(pack((values,), parts, held, n_dev), axes, split_axis=0, c...  3.86 us
  transfers between devices with their start and end apart: 2, of which 2 were waited for; matrix products, arithmetic and copies ran while one was open for 0% of the time, Pallas kernels for 10%

profile of v4, /device:TPU:1, one launch (start us, length us, event | category | flops | bytes accessed | tf_op | source)
XLA Modules:
  0.0 78.9 jit_solution(12914226637439559160)
XLA Ops:
  0.0 0.0 copy-start.3
  0.0 0.0 copy-start.5
  0.0 0.0 copy-start.4
  0.0 0.0 copy-start.2
  0.0 2.2 %pack.2 = bf16[32,2,64,128]{3,2,1,0:T(8,128)(2,1)} custom-call(bf16[64,3072]{1,0:T(8,128)(2,1)} %refs_0_.2, bf16[64,3072]{1,0:T(8,128)(2,1)} %refs_1_.1), custom_call_target="tpu_custom_call" | custom-call | bytes 1966080 | tf_op jit(solution)/shard_map/pack/pallas_call | solution.py:121
  2.3 7.1 %all-to-all-start = ((bf16[32,2,64,128]{3,2,1,0:T(8,128)(2,1)}), bf16[32,2,64,128]{3,2,1,0:T(8,128)(2,1)S(1)}, u32[]{:S(2)}, u32[]{:S(2)}) async-start(bf16[32,2,64,128]{3,2,1,0:T(8,128)(2,1)} %pack.2), calls=%async_computation | async-start | bytes 2097152 | tf_op jit(solution)/shard_map/all_to_all | solution.py:224
  9.4 1.9 %pack.3 = bf16[32,1,64,128]{3,2,1,0:T(8,128)(2,1)} custom-call(bf16[64,3072]{1,0:T(8,128)(2,1)} %refs_0_.3), custom_call_target="tpu_custom_call" | custom-call | bytes 983040 | tf_op jit(solution)/shard_map/pack/pallas_call | solution.py:121
  11.3 24.1 %all-to-all-done.got_ref = bf16[32,2,64,128]{3,2,1,0:T(8,128)(2,1)S(1)} async-done(((bf16[32,2,64,128]{3,2,1,0:T(8,128)(2,1)}), bf16[32,2,64,128]{3,2,1,0:T(8,128)(2,1)S(1)}, u32[]{:S(2)}, u32[]{:S(2)}) %all-to-all-start) | async-done | bytes 1048608 | tf_op jit(solution)/shard_map/all_to_all | solution.py:224
  35.4 3.9 %all-to-all-start.1 = ((bf16[32,1,64,128]{3,2,1,0:T(8,128)(2,1)}), bf16[32,1,64,128]{3,2,1,0:T(8,128)(2,1)S(1)}, u32[]{:S(2)}, u32[]{:S(2)}) async-start(bf16[32,1,64,128]{3,2,1,0:T(8,128)(2,1)} %pack.3), calls=%async_computation.1 | async-start | bytes 1048576 | tf_op jit(solution)/shard_map/all_to_all | solution.py:225
  39.3 0.1 pad_add_fusion.place_ref
  39.3 0.0 copy-done.3
  39.3 0.0 copy-done.5
  39.3 5.6 %weights.1 = (bf16[10,512,512]{2,1,0:T(8,128)(2,1)S(1)}, f32[4,512,128]{2,1,0:T(8,128)S(1)}) custom-call(s32[4]{0:T(128)S(1)} %copy-done.3, s32[4,4]{1,0:T(4,128)S(1)} %copy-done.5, s32[2]{0:T(128)S(1)} %pad_add_fusion.place_ref, bf16[32,2,64,128]{3,2,1,0:T(8,128)(2,1)S(1)} %all-to-all-done.got_ref), custom_call_target="tpu_custom_call" | custom-call | flops 671088640 | bytes 10485760 | tf_op jit(solution)/shard_map/weights/pallas_call | solution.py:229
  44.9 0.0 copy-start
  44.9 2.3 %copy-done = bf16[10,512,512]{2,1,0:T(8,128)(2,1)} copy-done((bf16[10,512,512]{2,1,0:T(8,128)(2,1)}, bf16[10,512,512]{2,1,0:T(8,128)(2,1)S(1)}, u32[]{:S(2)}) %copy-start) | copy-done | bytes 5242904
  47.2 7.8 %all-to-all-done.1.v_ref = bf16[32,1,64,128]{3,2,1,0:T(8,128)(2,1)S(1)} async-done(((bf16[32,1,64,128]{3,2,1,0:T(8,128)(2,1)}), bf16[32,1,64,128]{3,2,1,0:T(8,128)(2,1)S(1)}, u32[]{:S(2)}, u32[]{:S(2)}) %all-to-all-start.1) | async-done | bytes 524320 | tf_op jit(solution)/shard_map/all_to_all | solution.py:225
  55.0 0.0 copy-done.4
  55.0 0.0 copy-done.2
  55.1 0.0 copy-start.1
  55.1 2.5 %copy-done.1 = bf16[10,512,512]{2,1,0:T(8,128)(2,1)S(1)} copy-done((bf16[10,512,512]{2,1,0:T(8,128)(2,1)S(1)}, bf16[10,512,512]{2,1,0:T(8,128)(2,1)}, u32[]{:S(2)}) %copy-start.1) | copy-done | bytes 5242904
  57.5 2.1 %mix.1 = bf16[32,64,128]{2,1,0:T(8,128)(2,1)S(1)} custom-call(s32[4]{0:T(128)S(1)} %copy-done.3, s32[4]{0:T(128)S(1)} %copy-done.4, s32[2]{0:T(128)S(1)} %pad_add_fusion.place_ref, bf16[10,512,512]{2,1,0:T(8,128)(2,1)S(1)} %copy-done.1, f32[4,512,128]{2,1,0:T(8,128)S(1)} %get-tuple-element.8.total_ref, bf16[32,1,64,128]{3,2,1,0:T(8,128)(2,1)S(1)} %all-to-all-done.1.v_ref, ...), custom_call_target="tpu_custom_call" | custom-call | flops 671088640 | bytes 5242880 | tf_op jit(solution)/shard_map/mix/pallas_call | solution.py:241
  59.6 18.4 %all_to_all.15.in_ref = bf16[32,64,128]{2,1,0:T(8,128)(2,1)S(1)} all-to-all(bf16[32,64,128]{2,1,0:T(8,128)(2,1)S(1)} %mix.1), channel_id=1, replica_groups=mesh['seq'=16,'head'=2] {'seq','head'}, dimensions={0} | all-to-all | bytes 1048576 | tf_op jit(solution)/shard_map/all_to_all | solution.py:250
  78.1 0.8 %unpack.1 = bf16[64,3072]{1,0:T(8,128)(2,1)} custom-call(bf16[32,64,128]{2,1,0:T(8,128)(2,1)S(1)} %all_to_all.15.in_ref), custom_call_target="tpu_custom_call" | custom-call | tf_op jit(solution)/shard_map/unpack/pallas_call | solution.py:251
Async XLA Ops:
  0.0 39.3 %copy-start.3 = (s32[4]{0:T(128)S(1)}, s32[4]{0:T(128)}, u32[]{:S(2)}) copy-start(s32[4]{0:T(128)} %counts_ref.3) | copy-start | bytes 52
  0.0 39.3 %copy-start.5 = (s32[4,4]{1,0:T(4,128)S(1)}, s32[4,4]{1,0:T(4,128)}, u32[]{:S(2)}) copy-start(s32[4,4]{1,0:T(4,128)} %mask_ref.1) | copy-start | bytes 196
  0.0 55.0 %copy-start.4 = (s32[4]{0:T(128)S(1)}, s32[4]{0:T(128)}, u32[]{:S(2)}) copy-start(s32[4]{0:T(128)} %plan_ref.1) | copy-start | bytes 52
  0.0 55.0 %copy-start.2 = (f32[8,3072]{1,0:T(8,128)S(1)}, f32[8,3072]{1,0:T(8,128)}, u32[]{:S(2)}) copy-start(f32[8,3072]{1,0:T(8,128)} %gate_ref.1) | copy-start | bytes 294916
  2.3 33.1 %all-to-all-start = ((bf16[32,2,64,128]{3,2,1,0:T(8,128)(2,1)}), bf16[32,2,64,128]{3,2,1,0:T(8,128)(2,1)S(1)}, u32[]{:S(2)}, u32[]{:S(2)}) async-start(bf16[32,2,64,128]{3,2,1,0:T(8,128)(2,1)} %pack.2), calls=%async_computation | async-start | bytes 2097152 | tf_op jit(solution)/shard_map/all_to_all | solution.py:224
  35.4 19.7 %all-to-all-start.1 = ((bf16[32,1,64,128]{3,2,1,0:T(8,128)(2,1)}), bf16[32,1,64,128]{3,2,1,0:T(8,128)(2,1)S(1)}, u32[]{:S(2)}, u32[]{:S(2)}) async-start(bf16[32,1,64,128]{3,2,1,0:T(8,128)(2,1)} %pack.3), calls=%async_computation.1 | async-start | bytes 1048576 | tf_op jit(solution)/shard_map/all_to_all | solution.py:225
  44.9 2.3 %copy-start = (bf16[10,512,512]{2,1,0:T(8,128)(2,1)}, bf16[10,512,512]{2,1,0:T(8,128)(2,1)S(1)}, u32[]{:S(2)}) copy-start(bf16[10,512,512]{2,1,0:T(8,128)(2,1)S(1)} %get-tuple-element.7.weights_ref) | copy-start | bytes 15728644
  55.1 2.5 %copy-start.1 = (bf16[10,512,512]{2,1,0:T(8,128)(2,1)S(1)}, bf16[10,512,512]{2,1,0:T(8,128)(2,1)}, u32[]{:S(2)}) copy-start(bf16[10,512,512]{2,1,0:T(8,128)(2,1)} %copy-done) | copy-start | bytes 15728644

commit v5 on v2

--- a/solution.py
+++ b/solution.py
@@ -97,16 +97,37 @@
     return lax.all_to_all(result, "head", split_axis=0, concat_axis=1, tiled=True)
 
 
-def pack_kernel(parts, held, q_ref, k_ref, v_ref, out_ref):
+def pack_kernel(parts, held, *refs):
+    count = (len(refs) - 2) // 2
+    in_refs, out_ref, bufs, sems = refs[:count], refs[count], refs[count + 1 : -1], refs[-1]
     slots = out_ref.shape[0] // parts
-    for p in range(parts):
-        for s in range(slots):
-            for i, ref in enumerate((q_ref, k_ref, v_ref)):
-                if s < held:
-                    h = p * held + s
-                    out_ref[p * slots + s, i] = ref[:, h * HEAD_DIM : (h + 1) * HEAD_DIM]
-                else:
-                    out_ref[p * slots + s, i] = jnp.zeros(out_ref.shape[2:], out_ref.dtype)
+    copies = [pltpu.make_async_copy(in_refs[i], bufs[i], sems.at[i]) for i in range(count)]
+    for copy in copies:
+        copy.start()
+    for s in range(held, slots):
+        for p in range(parts):
+            out_ref[p * slots + s] = jnp.zeros(out_ref.shape[1:], out_ref.dtype)
+    for i, copy in enumerate(copies):
+        copy.wait()
+        for p in range(parts):
+            for s in range(held):
+                h = p * held + s
+                out_ref[p * slots + s, i] = bufs[i][:, h * HEAD_DIM : (h + 1) * HEAD_DIM]
+
+
+def pack(arrays, parts, held, n_dev):
+    local, feat = arrays[0].shape
+    count = len(arrays)
+    return pl.pallas_call(
+        functools.partial(pack_kernel, parts, held),
+        out_shape=jax.ShapeDtypeStruct((n_dev, count, local, HEAD_DIM), jnp.bfloat16),
+        in_specs=[pl.BlockSpec(memory_space=pl.ANY)] * count,
+        out_specs=pl.BlockSpec(memory_space=pltpu.VMEM),
+        scratch_shapes=[pltpu.VMEM((local, feat), jnp.bfloat16)] * count + [pltpu.SemaphoreType.DMA((count,))],
+        compiler_params=pltpu.CompilerParams(vmem_limit_bytes=60 * 1024 * 1024),
+        cost_estimate=pl.CostEstimate(flops=0, bytes_accessed=count * local * feat * 5, transcendentals=0),
+        name="pack",
+    )(*arrays)
 
 
 def unpack_kernel(parts, held, in_ref, out_ref):
@@ -117,7 +138,7 @@
             out_ref[:, h * HEAD_DIM : (h + 1) * HEAD_DIM] = in_ref[p * slots + s]
 
 
-def attention_kernel(block, counts_ref, plan_ref, mask_ref, place_ref, got_ref, gate_ref, out_ref):
+def attention_kernel(block, counts_ref, plan_ref, mask_ref, place_ref, got_ref, gate_ref, out_ref, bias_ref):
     n_dev, _, local, _ = got_ref.shape
     per_group = n_dev // GROUPS
     group_tok = per_group * local
@@ -130,34 +151,49 @@
     def _():
         gates = gate_ref[:, pl.ds(pl.multiple_of(head * HEAD_DIM, HEAD_DIM), HEAD_DIM)]
         level = lax.broadcasted_iota(jnp.int32, (LEVELS, HEAD_DIM), 0)
-        for c in range(GROUPS):
-            width = (c + 1) * group_tok
-            column = lax.broadcasted_iota(jnp.int32, (1, group_tok), 1)
-            limits = [counts_ref[d] * mask_ref[c, d] for d in range(c + 1)]
-            allowed = jnp.concatenate([column < limits[d] for d in range(c + 1)], axis=1)
+        place = lax.broadcasted_iota(jnp.int32, (group_tok, HEAD_DIM), 0)
+        for d in range(GROUPS):
+            bias_ref[d] = jnp.where(place < counts_ref[d], 0.0, -1e30).astype(jnp.bfloat16)
+        lane = lax.broadcasted_iota(jnp.int32, (rows, HEAD_DIM), 1)
+        one = jnp.where(lane == 0, 1.0, 0.0).astype(jnp.bfloat16)
+        ones = jnp.ones((group_tok, HEAD_DIM), jnp.bfloat16)
+
+        def group_rows(c, seen):
             gate = jnp.sum(jnp.where(level == plan_ref[c], gates, jnp.float32(0.0)), axis=0, keepdims=True)
 
             @pl.loop(0, per_group // block)
             def _(step):
                 first = c * per_group + step * block
-                scores = lax.dot_general(
-                    got_ref[pl.ds(first, block), 0].reshape(rows, HEAD_DIM),
-                    got_ref[: (c + 1) * per_group, 1].reshape(width, HEAD_DIM),
-                    (((1,), (1,)), ((), ())),
-                    preferred_element_type=jnp.float32,
-                )
-                scores = jnp.where(allowed, scores, jnp.float32(-1e30))
-                top = jnp.max(scores, axis=1, keepdims=True)
-                weights = jnp.exp2(scores * factor - top * factor)
-                total = jnp.sum(weights, axis=1, keepdims=True)
-                mixed = jnp.dot(
-                    weights.astype(jnp.bfloat16),
-                    got_ref[: (c + 1) * per_group, 2].reshape(width, HEAD_DIM),
-                    preferred_element_type=jnp.float32,
-                )
+                q = jnp.concatenate([got_ref[pl.ds(first, block), 0].reshape(rows, HEAD_DIM), one], axis=1)
+                scores = []
+                for d in seen:
+                    k = got_ref[d * per_group : (d + 1) * per_group, 1].reshape(group_tok, HEAD_DIM)
+                    scores.append(
+                        lax.dot_general(
+                            q,
+                            jnp.concatenate([k, bias_ref[d]], axis=1),
+                            (((1,), (1,)), ((), ())),
+                            preferred_element_type=jnp.float32,
+                        )
+                    )
+                top = functools.reduce(jnp.maximum, [jnp.max(s, axis=1, keepdims=True) for s in scores])
+                mixed = jnp.zeros((rows, 2 * HEAD_DIM), jnp.float32)
+                for d, s in zip(seen, scores):
+                    weights = jnp.exp2(s * factor - top * factor).astype(jnp.bfloat16)
+                    v = got_ref[d * per_group : (d + 1) * per_group, 2].reshape(group_tok, HEAD_DIM)
+                    mixed += jnp.dot(
+                        weights, jnp.concatenate([v, ones], axis=1), preferred_element_type=jnp.float32
+                    )
                 position = step * rows + lax.broadcasted_iota(jnp.int32, (rows, 1), 0)
-                mixed = jnp.where(position < counts_ref[c], mixed / total * gate, jnp.float32(0.0))
+                mixed = mixed[:, :HEAD_DIM] / mixed[:, HEAD_DIM:] * gate
+                mixed = jnp.where(position < counts_ref[c], mixed, jnp.float32(0.0))
                 out_ref[pl.ds(first, block)] = mixed.astype(jnp.bfloat16).reshape(block, local, HEAD_DIM)
+
+        for c in range(GROUPS):
+            pattern = sum((mask_ref[c, d] * 2**d for d in range(c)), jnp.int32(0))
+            for bits in range(2**c):
+                seen = [d for d in range(c) if bits >> d & 1] + [c]
+                pl.when(pattern == bits)(functools.partial(group_rows, c, seen))
 
     @pl.when(busy == 0)
     def _():
@@ -179,20 +215,14 @@
     smem = pl.BlockSpec(memory_space=pltpu.SMEM)
     vmem = pl.BlockSpec(memory_space=pltpu.VMEM)
 
-    sent = pl.pallas_call(
-        functools.partial(pack_kernel, parts, held),
-        out_shape=jax.ShapeDtypeStruct((n_dev, 3, local, HEAD_DIM), jnp.bfloat16),
-        in_specs=[vmem] * 3,
-        out_specs=vmem,
-        compiler_params=pltpu.CompilerParams(vmem_limit_bytes=16 * 1024 * 1024),
-        name="pack",
-    )(queries, keys, values)
+    sent = pack((queries, keys, values), parts, held, n_dev)
     got = lax.all_to_all(sent, axes, split_axis=0, concat_axis=0, tiled=True)
     result = pl.pallas_call(
         functools.partial(attention_kernel, max(1, 256 // local)),
         out_shape=jax.ShapeDtypeStruct((n_dev, local, HEAD_DIM), jnp.bfloat16),
         in_specs=[smem, smem, smem, smem, vmem, vmem],
         out_specs=vmem,
+        scratch_shapes=[pltpu.VMEM((GROUPS, n_dev * local // GROUPS, HEAD_DIM), jnp.bfloat16)],
         compiler_params=pltpu.CompilerParams(vmem_limit_bytes=40 * 1024 * 1024),
         name="attention",
     )(counts, plan, group_mask, place, got, gate_table)

time: 76.5 us -> 74.9 us (0.979)
  local copies, waits for them, and re-layouts: 3 us -> 0.03 us
  Pallas kernels: 9.28 us -> 11.2 us
    unnamed x14 -> x8, local copies, waits for them, and re-layouts: 3 us -> 0.03 us
    pallas_call x1, Pallas kernels: 1.39 us -> 2.48 us  [pack(): pl.pallas_call(functools.partial(pack_kernel, parts, held), out_shape=jax...]
    pallas_call x1, Pallas kernels: 7.07 us -> 7.94 us  [head_each(): pl.pallas_call(functools.partial(attention_kernel, max(1, 256 // local)),...]
where the time goes in v5:
time: 74.9 us; the launch traced here: 75.2 us
  waiting for transfers between devices  36.8 us (49%)
  blocking collectives  19.9 us (27%)
  Pallas kernels  11.2 us (15%)
  starting transfers between devices  7.1 us (9%)
    all_to_all x1, waiting for transfers between devices, head_each(): got = lax.all_to_all(sent, axes, split_axis=0, concat_axis=0, tiled=True)  36.8 us
    all_to_all x1, blocking collectives, head_each(): back = lax.all_to_all(result, axes, split_axis=0, concat_axis=0, tiled=True)  19.9 us
    pallas_call x1, Pallas kernels, head_each(): pl.pallas_call(functools.partial(attention_kernel, max(1, 256 // local)),...  7.94 us
    all_to_all x1, starting transfers between devices, head_each(): got = lax.all_to_all(sent, axes, split_axis=0, concat_axis=0, tiled=True)  7.1 us
    pallas_call x1, Pallas kernels, pack(): pl.pallas_call(functools.partial(pack_kernel, parts, held), out_shape=jax...  2.48 us
  transfers between devices with their start and end apart: 1, of which 1 were waited for; matrix products, arithmetic and copies ran while one was open for 0% of the time, Pallas kernels for 0%

profile of v5, /device:TPU:1, one launch (start us, length us, event | category | flops | bytes accessed | tf_op | source)
XLA Modules:
  0.0 75.2 jit_solution(5192487280210017538)
XLA Ops:
  0.0 2.5 %pack.1 = bf16[32,3,64,128]{3,2,1,0:T(8,128)(2,1)} custom-call(bf16[64,3072]{1,0:T(8,128)(2,1)} %refs_0_.1, bf16[64,3072]{1,0:T(8,128)(2,1)} %refs_1_.1, bf16[64,3072]{1,0:T(8,128)(2,1)} %refs_2_.1), custom_call_target="tpu_custom_call" | custom-call | bytes 2949120 | tf_op jit(solution)/shard_map/pack/pallas_call | solution.py:121
  2.5 0.0 copy-start
  2.5 0.0 copy-start.1
  2.5 0.0 copy-start.2
  2.5 0.0 copy-start.3
  2.5 7.1 %all-to-all-start = ((bf16[32,3,64,128]{3,2,1,0:T(8,128)(2,1)}), bf16[32,3,64,128]{3,2,1,0:T(8,128)(2,1)S(1)}, u32[]{:S(2)}, u32[]{:S(2)}) async-start(bf16[32,3,64,128]{3,2,1,0:T(8,128)(2,1)} %pack.1), calls=%async_computation | async-start | bytes 3145728 | tf_op jit(solution)/shard_map/all_to_all | solution.py:219
  9.7 0.1 pad_add_fusion.place_ref
  9.8 36.8 %all-to-all-done.got_ref = bf16[32,3,64,128]{3,2,1,0:T(8,128)(2,1)S(1)} async-done(((bf16[32,3,64,128]{3,2,1,0:T(8,128)(2,1)}), bf16[32,3,64,128]{3,2,1,0:T(8,128)(2,1)S(1)}, u32[]{:S(2)}, u32[]{:S(2)}) %all-to-all-start) | async-done | bytes 1572896 | tf_op jit(solution)/shard_map/all_to_all | solution.py:219
  46.5 0.0 copy-done
  46.5 0.0 copy-done.1
  46.5 0.0 copy-done.2
  46.5 0.0 copy-done.3
  46.5 7.9 %attention.1 = bf16[32,64,128]{2,1,0:T(8,128)(2,1)S(1)} custom-call(s32[4]{0:T(128)S(1)} %copy-done.2, s32[4]{0:T(128)S(1)} %copy-done.3, s32[4,4]{1,0:T(4,128)S(1)} %copy-done.1, s32[2]{0:T(128)S(1)} %pad_add_fusion.place_ref, bf16[32,3,64,128]{3,2,1,0:T(8,128)(2,1)S(1)} %all-to-all-done.got_ref, f32[8,3072]{1,0:T(8,128)S(1)} %copy-done), custom_call_target="tpu_custom_call" | custom-call | tf_op jit(solution)/shard_map/attention/pallas_call | solution.py:220
  54.5 19.9 %all_to_all.10.in_ref = bf16[32,64,128]{2,1,0:T(8,128)(2,1)S(1)} all-to-all(bf16[32,64,128]{2,1,0:T(8,128)(2,1)S(1)} %attention.1), channel_id=1, replica_groups=mesh['seq'=16,'head'=2] {'seq','head'}, dimensions={0} | all-to-all | bytes 1048576 | tf_op jit(solution)/shard_map/all_to_all | solution.py:229
  74.3 0.8 %unpack.1 = bf16[64,3072]{1,0:T(8,128)(2,1)} custom-call(bf16[32,64,128]{2,1,0:T(8,128)(2,1)S(1)} %all_to_all.10.in_ref), custom_call_target="tpu_custom_call" | custom-call | tf_op jit(solution)/shard_map/unpack/pallas_call | solution.py:230
Async XLA Ops:
  2.5 44.0 %copy-start = (f32[8,3072]{1,0:T(8,128)S(1)}, f32[8,3072]{1,0:T(8,128)}, u32[]{:S(2)}) copy-start(f32[8,3072]{1,0:T(8,128)} %gate_ref.1) | copy-start | bytes 294916
  2.5 44.0 %copy-start.1 = (s32[4,4]{1,0:T(4,128)S(1)}, s32[4,4]{1,0:T(4,128)}, u32[]{:S(2)}) copy-start(s32[4,4]{1,0:T(4,128)} %mask_ref.1) | copy-start | bytes 196
  2.5 44.0 %copy-start.2 = (s32[4]{0:T(128)S(1)}, s32[4]{0:T(128)}, u32[]{:S(2)}) copy-start(s32[4]{0:T(128)} %counts_ref.1) | copy-start | bytes 52
  2.5 44.0 %copy-start.3 = (s32[4]{0:T(128)S(1)}, s32[4]{0:T(128)}, u32[]{:S(2)}) copy-start(s32[4]{0:T(128)} %plan_ref.1) | copy-start | bytes 52
  2.5 44.0 %all-to-all-start = ((bf16[32,3,64,128]{3,2,1,0:T(8,128)(2,1)}), bf16[32,3,64,128]{3,2,1,0:T(8,128)(2,1)S(1)}, u32[]{:S(2)}, u32[]{:S(2)}) async-start(bf16[32,3,64,128]{3,2,1,0:T(8,128)(2,1)} %pack.1), calls=%async_computation | async-start | bytes 3145728 | tf_op jit(solution)/shard_map/all_to_all | solution.py:219
